TPU v7x, 32 devices: a whole 2x2x4 slice. The times are simulated.
32 devices in a mesh: cons: 4 (over y, core), ty: 2 (over x), tx: 4 (over z).
Axes of the slice: x: 2, y: 2, z: 4, core: 2. Of those that a mesh axis runs over, the one named last changes fastest.
Arguments:
- elevation: float32 [8, 2, 288, 2048], P('cons', None, 'ty', 'tx'), may hold values from -6 to 6
- equilibrium: float32 [8, 2, 288, 2048], P('cons', None, 'ty', 'tx'), may hold values from -5 to 5
- depth: float32 [288, 2048], P('ty', 'tx'), may hold values from 0.1 to 1
- land_mask: int32 [288, 2048], P('ty', 'tx'), may hold values 0 or 1
- friction_prev: float32 [288, 2048], P('ty', 'tx'), may hold values from 0.3 to 3
Outputs:
- elevation_out: float32 [8, 2, 288, 2048], P('cons', None, 'ty', 'tx')
- friction: float32 [288, 2048], P('ty', 'tx')
All inputs are finite; a program needn't handle non-finite values. No bound on the sum of `land_mask` on one device may be relied on, other than what follows from the above.
Results may differ from a plain program's by a relative error of at most 0.00002.
Values sent between devices are 32-bit elements; how exact they have to be, the bound alone decides.
No kernel may reach another device: no remote copies, remote signals or barrier semaphores. Data moves between devices by JAX's collectives and lax.ppermute only.
A program may use at most 64 MiB of HBM per device.

v0:
```python
import functools
import math

import jax
import jax.numpy as jnp
from jax import lax
from jax.experimental import pallas as pl
from jax.experimental.pallas import tpu as pltpu
from jax.sharding import PartitionSpec as P

OMEGA_TABLE = (1.0, 1.0351, 0.9582, 1.0379, 0.5181, 0.4816, 0.5164, 0.4454)
AY = 0.5
THETA = 0.05
DRAG = 0.5
BACKGROUND = 0.01
F32 = jnp.float32
LANES = 128
FIELDS = 6
MSG = 4 * FIELDS
TINY_DEPTH = 1e-6
PARAMS = pltpu.CompilerParams(vmem_limit_bytes=16 * 1024 * 1024)


def vmem(x):
    return pltpu.with_memory_space_constraint(x, pltpu.VMEM)


def hbm(x):
    return pltpu.with_memory_space_constraint(x, pltpu.HBM)


def recip(x):
    return pl.reciprocal(x, approx=True) if jnp.ndim(x) else 1.0 / x


def metric(rows, total):
    lat = (rows + 0.5) * (120.0 / total * math.pi / 180.0) - math.pi / 3.0
    s = lat * lat
    acc = jnp.full_like(s, 1.0 / math.factorial(16))
    for n in (14, 12, 10, 8, 6, 4, 2, 0):
        acc = ((-1.0) ** (n // 2)) / math.factorial(n) + s * acc
    return 0.5 / acc


def omegas(kdev):
    index = lax.axis_index("cons")
    out = []
    for c in range(kdev):
        w = jnp.float32(OMEGA_TABLE[c])
        for i in range(1, len(OMEGA_TABLE) // kdev):
            w = jnp.where(index == i, jnp.float32(OMEGA_TABLE[i * kdev + c]), w)
        out.append(w)
    return out


def rolled(x, shift, axis):
    return pltpu.roll(x, shift % x.shape[axis], axis)


def face(zr, zi, zr_next, zi_next, r2, coef, w2):
    g = coef * recip(r2 * r2 + w2 * w2)
    a = g * r2
    b = g * w2
    dr = zr - zr_next
    di = zi - zi_next
    return a * dr + b * di, a * di - b * dr


def flux(dr, di, g, a, w2):
    b = g * w2
    return a * dr + b * di, a * di - b * dr


def pack_kernel(e_in, q_in, d_in, m_in, r_in, e, q, d, m, r, m2, m1, mn, ms, ints, cols, sems):
    kdev, _, rows, width = e.shape
    copies = []

    def fetch(src, dst):
        copy = pltpu.make_async_copy(src, dst, sems.at[len(copies)])
        copy.start()
        copies.append(copy)

    for src, dst in ((d_in, d), (m_in, ints), (r_in, r)):
        fetch(src, dst)
    for c in range(kdev):
        for p in range(2):
            fetch(e_in.at[c, p], e.at[c, p])
            fetch(q_in.at[c, p], q.at[c, p])
    for copy in copies[:3]:
        copy.wait()
    m[...] = ints[...].astype(F32)
    for copy in copies[3:]:
        copy.wait()
    sides = (slice(0, LANES), slice(width - LANES, width))
    ends = (slice(0, 8), slice(rows - 8, rows))

    lane = lax.broadcasted_iota(jnp.int32, (rows, LANES), 1)
    both = jnp.zeros((rows, LANES), F32)
    for s in range(2):
        side = sides[s]
        planes = [e[c, p, :, side] - q[c, p, :, side] for p in range(2) for c in range(2)]
        planes += [r[:, side], d[:, side], m[:, side]]
        planes += [e[c, p, :, side] for p in range(2) for c in range(2)]
        for k, plane in enumerate(planes):
            at = 32 * s + 2 * k
            shift = at if s == 0 else at - (LANES - 2)
            both = jnp.where((lane == at) | (lane == at + 1), rolled(plane, shift, 1), both)
    pad = -(-rows // LANES) * LANES
    turned = jnp.concatenate([both, jnp.zeros((pad - rows, LANES), F32)], axis=0).T
    for s in range(2):
        at = 32 * s
        near = 0 if s == 0 else 1
        for g in range(2):
            for line in range(2):
                for c in range(2):
                    row = at + 4 * g + 2 * c + line
                    cols[s, 4 * g + 2 * line + c, :] = turned[row, :]
        for g in range(2, 5):
            for line in range(2):
                for c in range(2):
                    cols[s, 4 * g + 2 * line + c, :] = turned[at + 2 * (g + 2) + line, :]
        for c in range(4):
            cols[s, 20 + c, :] = turned[at + 2 * (7 + c) + near, :]
    odd = lax.rem(lax.axis_index("tx"), 2)
    m1[...] = cols[1 - odd]
    m2[:MSG, :] = cols[odd]
    m2[MSG:, :] = jnp.zeros((m2.shape[0] - MSG, m2.shape[1]), F32)

    for s, out in enumerate((ms, mn)):
        base = 0 if s == 0 else 6
        near = 0 if s == 0 else 7
        out[:, width:] = jnp.zeros((MSG, LANES), F32)
        for p in range(2):
            for c in range(2):
                line8 = e[c, p, ends[s], :]
                z = line8 - q[c, p, ends[s], :]
                for line in range(2):
                    out[4 * p + 2 * line + c, :width] = z[base + line, :]
                out[20 + 2 * p + c, :width] = line8[near, :]
        for g, plane in ((2, r[ends[s], :]), (3, d[ends[s], :]), (4, m[ends[s], :])):
            for line in range(2):
                for c in range(2):
                    out[4 * g + 2 * line + c, :width] = plane[base + line, :]


def pack(elevation, equilibrium, depth, land_mask, friction):
    kdev, _, rows, width = elevation.shape
    pad = -(-rows // LANES) * LANES
    field, plane = pltpu.VMEM(elevation.shape, F32), pltpu.VMEM(depth.shape, F32)
    row = pltpu.VMEM((MSG, width + LANES), F32)
    return pl.pallas_call(
        pack_kernel,
        out_shape=(field, field, plane, plane, plane, pltpu.VMEM((MSG + 8, pad), F32), pltpu.VMEM((MSG, pad), F32), row, row),
        in_specs=[pl.BlockSpec(memory_space=pltpu.HBM)] * 5,
        out_specs=[pl.BlockSpec(memory_space=pltpu.VMEM)] * 9,
        scratch_shapes=[
            pltpu.VMEM(depth.shape, jnp.int32),
            pltpu.VMEM((2, MSG, pad), F32),
            pltpu.SemaphoreType.DMA((3 + 4 * kdev,)),
        ],
        compiler_params=PARAMS,
        name="pack",
    )(*map(hbm, (elevation, equilibrium, depth, land_mask, friction)))


def tile_rows(ref, at, size, nxt):
    here = ref[at : at + size, :]
    after = ref[nxt : nxt + 8, :]
    return here, jnp.concatenate([here[1:], after[0:1]], axis=0)


def east(x):
    return rolled(x, -1, 1)


def row_metric(at, size, width, rows):
    first = lax.axis_index("ty") * rows
    index = lax.broadcasted_iota(jnp.int32, (size, LANES), 0) + (first + at)
    ax = metric(index.astype(F32), rows * lax.axis_size("ty"))
    return ax, jnp.concatenate([ax] * (width // LANES), axis=1)


def first_kernel(e, q, d, mask, r, after, e1, send, keep, var):
    del after
    kdev, _, rows, width = e.shape
    size = 16
    ws = omegas(kdev)
    last_v = [jnp.zeros((1, width), F32)] * (2 * kdev)
    for at in range(0, rows, size):
        nxt = min(at + size, rows - 8)
        _, ax = row_metric(at, size, width, rows)
        md, mn = tile_rows(mask, at, size, nxt)
        dd, dn = tile_rows(d, at, size, nxt)
        rd, rn = tile_rows(r, at, size, nxt)
        coef_u = (THETA * ax * ax) * (md * east(md) * (dd + east(dd)))
        coef_v = (THETA * AY * AY) * (md * mn * (dd + dn))
        r2u = rd + east(rd)
        r2v = rd + rn
        squ, sqv = r2u * r2u, r2v * r2v
        sum_u = sum_v = None
        for c in range(kdev):
            w2 = 2.0 * ws[c]
            wt = THETA * ws[c]
            er, ern = tile_rows(e.at[c, 0], at, size, nxt)
            ei, ein = tile_rows(e.at[c, 1], at, size, nxt)
            qr, qrn = tile_rows(q.at[c, 0], at, size, nxt)
            qi, qin = tile_rows(q.at[c, 1], at, size, nxt)
            zr, zi = er - qr, ei - qi
            gu = coef_u * recip(squ + w2 * w2)
            gv = coef_v * recip(sqv + w2 * w2)
            ur, ui = flux(zr - east(zr), zi - east(zi), gu, gu * r2u, w2)
            vr, vi = flux(zr - (ern - qrn), zi - (ein - qin), gv, gv * r2v, w2)
            uwr, uwi = rolled(ur, 1, 1), rolled(ui, 1, 1)
            vsr = jnp.concatenate([last_v[2 * c], vr[:-1]], axis=0)
            vsi = jnp.concatenate([last_v[2 * c + 1], vi[:-1]], axis=0)
            last_v[2 * c], last_v[2 * c + 1] = vr[-1:], vi[-1:]
            e1[c, 0, at : at + size, :] = md * (er + wt * ei - (ur - uwr) - (vr - vsr))
            e1[c, 1, at : at + size, :] = md * (ei - wt * er - (ui - uwi) - (vi - vsi))
            su = (ur + uwr) * (ur + uwr) + (ui + uwi) * (ui + uwi)
            sv = (vr + vsr) * (vr + vsr) + (vi + vsi) * (vi + vsi)
            sum_u = su if sum_u is None else sum_u + su
            sum_v = sv if sum_v is None else sum_v + sv
        inv = recip(dd)
        ia = recip(THETA * ax)
        total = (0.125 * ia * ia) * sum_u + (0.125 / (THETA * AY) ** 2) * sum_v
        var[at : at + size, :] = total * (inv * inv)
    half = rows // 2
    core = lax.rem(lax.axis_index("cons"), 2)
    send[...] = var[pl.ds(pl.multiple_of((1 - core) * half, 8), half), :]
    keep[...] = var[pl.ds(pl.multiple_of(core * half, 8), half), :]


def first_sweep(e, q, d, m, r, after):
    kdev, _, rows, width = e.shape
    half = pltpu.VMEM((rows // 2, width), F32)
    return pl.pallas_call(
        first_kernel,
        out_shape=(pltpu.VMEM(e.shape, F32), half, half),
        in_specs=[pl.BlockSpec(memory_space=pltpu.VMEM)] * 6,
        out_specs=[pl.BlockSpec(memory_space=pltpu.VMEM)] * 3,
        scratch_shapes=[pltpu.VMEM(d.shape, F32)],
        compiler_params=PARAMS,
        cost_estimate=pl.CostEstimate(flops=80 * e.size, bytes_accessed=160 * e.size, transcendentals=0),
        name="first_sweep",
    )(*map(vmem, (e, q, d, m, r, after)))


def add_kernel(a, b, *refs):
    refs[-1][...] = a[...] + b[...]


def added(a, b, *after):
    return pl.pallas_call(
        add_kernel,
        out_shape=pltpu.VMEM(a.shape, F32),
        in_specs=[pl.BlockSpec(memory_space=pltpu.VMEM)] * (2 + len(after)),
        out_specs=pl.BlockSpec(memory_space=pltpu.VMEM),
        compiler_params=PARAMS,
        name="added",
    )(vmem(a), vmem(b), *map(vmem, after))


def halves_kernel(a, b, after, left, right):
    del after
    cut = left.shape[1]
    left[...] = a[:, :cut] + b[:, :cut]
    right[...] = a[:, cut:] + b[:, cut:]


def halves(a, b, after):
    part = pltpu.VMEM((a.shape[0], a.shape[1] // 2), F32)
    return pl.pallas_call(
        halves_kernel,
        out_shape=(part, part),
        in_specs=[pl.BlockSpec(memory_space=pltpu.VMEM)] * 3,
        out_specs=[pl.BlockSpec(memory_space=pltpu.VMEM)] * 2,
        compiler_params=PARAMS,
        name="halves",
    )(vmem(a), vmem(b), vmem(after))


def join_kernel(after, *refs):
    del after
    out = refs[-1]
    rows, cut = refs[0].shape
    for k, at in enumerate((slice(0, cut), slice(cut, 2 * cut))):
        out[:rows, at] = functools.reduce(jnp.add, [ref[...] for ref in refs[k:-1:3]])
    out[rows:, :] = functools.reduce(jnp.add, [ref[...] for ref in refs[2:-1:3]])


def joined(parts, after):
    (rows, cut), rims = parts[0][0].shape, parts[0][2].shape[0]
    flat = [x for part in parts for x in part]
    return pl.pallas_call(
        join_kernel,
        out_shape=pltpu.VMEM((rows + rims, 2 * cut), F32),
        in_specs=[pl.BlockSpec(memory_space=pltpu.VMEM)] * (1 + len(flat)),
        out_specs=pl.BlockSpec(memory_space=pltpu.VMEM),
        compiler_params=PARAMS,
        name="joined",
    )(*map(vmem, (after, *flat)))


def roles(a, b):
    even = lax.rem(lax.axis_index("tx"), 2) == 0
    return jnp.where(even, b, a), jnp.where(even, a, b)


def merge_kernel(rows, f2, f1, mn, ms, send, mn_out, ms_out, my_out, send_out):
    width = mn.shape[1] - LANES
    fw, fe = roles(f1[...], f2[:MSG, :])
    block = (rows - 1) // LANES * LANES
    lane = lax.broadcasted_iota(jnp.int32, (MSG, LANES), 1)
    in_block = rows - 1 - block
    fe_last = rolled(rolled(fe[:, block : block + LANES], -in_block, 1), 2, 0)
    fw_last = rolled(fw[:, block : block + LANES], LANES - 1 - in_block, 1)
    fe_first = fe[:, :LANES]
    fw_first = rolled(rolled(fw[:, :LANES], LANES - 1, 1), -2, 0)
    n_end = jnp.where(lane == 0, fe_last, jnp.where(lane == LANES - 1, fw_last, 0.0))
    s_end = jnp.where(lane == 0, fe_first, jnp.where(lane == LANES - 1, fw_first, 0.0))
    mn_out[:, :width] = mn[:, :width]
    ms_out[:, :width] = ms[:, :width]
    mn_out[:, width:] = n_end
    ms_out[:, width:] = s_end
    low = lax.axis_index("ty") == 0
    my_out[:MSG, :] = jnp.where(low, mn_out[...], ms_out[...])
    my_out[MSG:, :] = jnp.zeros((my_out.shape[0] - MSG, my_out.shape[1]), F32)
    send_out[...] = send[...]


def merge(rows, f1, f2, mn, ms, send):
    out = pltpu.VMEM(mn.shape, F32)
    return pl.pallas_call(
        functools.partial(merge_kernel, rows),
        out_shape=(out, out, pltpu.VMEM((MSG + 8, mn.shape[1]), F32), pltpu.VMEM(send.shape, F32)),
        in_specs=[pl.BlockSpec(memory_space=pltpu.VMEM)] * 5,
        out_specs=[pl.BlockSpec(memory_space=pltpu.VMEM)] * 4,
        compiler_params=PARAMS,
        name="merge",
    )(*map(vmem, (f2, f1, mn, ms, send)))


def strip_omega(shape, ws):
    odd = lax.rem(lax.broadcasted_iota(jnp.int32, shape, 0), 2)
    return jnp.where(odd == 0, ws[0], ws[1])


def strip_sweep(low, high, ws, g_across, g_along):
    field = [jnp.concatenate([low[4 * g : 4 * g + 4], high[4 * g : 4 * g + 4]], axis=0) for g in range(5)]
    zr, zi, r, d, m = field
    none = jnp.zeros((2, low.shape[1]), F32)
    er = jnp.concatenate([none, low[20:22], high[20:22], none], axis=0)
    ei = jnp.concatenate([none, low[22:24], high[22:24], none], axis=0)
    w = strip_omega(zr.shape, ws)
    w2 = 2.0 * w
    wt = THETA * w
    up = lambda x: rolled(x, -2, 0)
    nx = lambda x: rolled(x, -1, 1)
    coef_a = (THETA * g_across * g_across) * (m * up(m) * (d + up(d)))
    coef_l = (THETA * g_along * g_along) * (m * nx(m) * (d + nx(d)))
    ar, ai = face(zr, zi, up(zr), up(zi), r + up(r), coef_a, w2)
    lr, li = face(zr, zi, nx(zr), nx(zi), r + nx(r), coef_l, w2)
    abr, abi = rolled(ar, 2, 0), rolled(ai, 2, 0)
    lbr, lbi = rolled(lr, 1, 1), rolled(li, 1, 1)
    e1r = m * (er + wt * ei - (ar - abr) - (lr - lbr))
    e1i = m * (ei - wt * er - (ai - abi) - (li - lbi))
    sa = (ar + abr) * (ar + abr) + (ai + abi) * (ai + abi)
    sl = (lr + lbr) * (lr + lbr) + (li + lbi) * (li + lbi)
    inv = recip(jnp.maximum(d, TINY_DEPTH))
    ia = recip(THETA * g_across)
    il = recip(THETA * g_along)
    var = 0.125 * (ia * ia * sa + il * il * sl) * (inv * inv)
    var = var + rolled(var, -1, 0)
    z1r = e1r - (er - zr)
    z1i = e1i - (ei - zi)
    return (z1r, z1i, d, coef_a, e1r, e1i), var


def rim_kernel(rows, after, m2, m1, f2, f1, mn, ms, fn_ref, fs_ref, s_out, n_out, w_out, e_out, sums):
    kdev = 2
    width = mn.shape[1] - LANES
    pad = m1.shape[1]
    ws = omegas(kdev)
    ty, count = lax.axis_index("ty"), lax.axis_size("ty")
    first = (ty * rows).astype(F32)
    total = rows * count
    fn = jnp.where(ty < count - 1, fn_ref[:MSG, :], 0.0)
    fs = jnp.where(ty > 0, fs_ref[:MSG, :], 0.0)

    ay = AY
    line = lax.broadcasted_iota(jnp.int32, (8, LANES), 0) // 2
    for low, high, start, out, at in ((fs, ms[...], -2, s_out, 0), (mn[...], fn, rows - 2, n_out, 2)):
        ax = metric((line + start).astype(F32) + first, total)
        ax = jnp.concatenate([ax] * (low.shape[1] // LANES), axis=1)
        held, var = strip_sweep(low, high, ws, ay, ax)
        for k, x in enumerate(held):
            out[8 * k : 8 * k + 8, :] = x
        for p in range(2):
            sums[at + p, :] = var[2 + 2 * p, :width]

    mw, me = roles(m1[...], m2[:MSG, :])
    fw, fe = roles(f1[...], f2[:MSG, :])
    mw, me, fw, fe = mw, me, fw, fe
    hi = rows - (pad - LANES)
    lane = lax.broadcasted_iota(jnp.int32, (MSG, LANES), 1)
    fn_end, fn_lo, fn_hi = fn[:, width:], fn[:, :LANES], fn[:, width - LANES : width]
    fs_end, fs_lo, fs_hi = fs[:, width:], fs[:, :LANES], fs[:, width - LANES : width]
    down = lambda x: rolled(x, 2, 0)
    up = lambda x: rolled(x, -2, 0)

    def ended(msg, north, north_lane, south, south_lane):
        block = msg[:, pad - LANES :]
        block = jnp.where(lane == hi, rolled(north, hi - north_lane, 1), block)
        block = jnp.where(lane == LANES - 1, rolled(south, LANES - 1 - south_lane, 1), block)
        return jnp.concatenate([msg[:, : pad - LANES], block], axis=1)

    last = LANES - 1
    low_w = ended(fw, down(fn_end), last, fs_end, last)
    high_w = ended(mw, fn_lo, 0, up(fs_lo), 0)
    low_e = ended(me, down(fn_hi), last, fs_hi, last)
    high_e = ended(fe, fn_end, 0, up(fs_end), 0)
    row = lax.broadcasted_iota(jnp.int32, (8, pad), 1).astype(F32) + first
    ax = metric(jnp.minimum(row, first + rows), total)
    for low, high, out, at in ((low_w, high_w, w_out, 4), (low_e, high_e, e_out, 5)):
        held, var = strip_sweep(low, high, ws, ax, ay)
        for k, x in enumerate(held):
            out[8 * k : 8 * k + 8, :] = x
        for p in range(2):
            sums[at, p * pad : (p + 1) * pad] = var[2 + 2 * p, :]
    sums[6:, :] = jnp.zeros((2, width), F32)


def rim(rows, m1, m2, f1, f2, mn, ms, fn, fs, after):
    row = pltpu.VMEM((48, mn.shape[1]), F32)
    col = pltpu.VMEM((48, m1.shape[1]), F32)
    sums = pltpu.VMEM((8, mn.shape[1] - LANES), F32)
    return pl.pallas_call(
        functools.partial(rim_kernel, rows),
        out_shape=(row, row, col, col, sums),
        in_specs=[pl.BlockSpec(memory_space=pltpu.VMEM)] * 9,
        out_specs=[pl.BlockSpec(memory_space=pltpu.VMEM)] * 5,
        compiler_params=PARAMS,
        name="rim",
    )(*map(vmem, (after, m2, m1, f2, f1, mn, ms, fn, fs)))


def prepare_kernel(e1_in, q, d, m, ss, sn, sw, se, du, dv, base, coef, e1, cols):
    kdev, _, rows, width = e1_in.shape
    size = 16
    ws = omegas(kdev)
    e1[...] = e1_in[...]
    for p in range(2):
        cols[2 * p : 2 * p + 2, :] = sw[8 * (4 + p) + 4 : 8 * (4 + p) + 6, :]
        cols[4 + 2 * p : 6 + 2 * p, :] = se[8 * (4 + p) + 2 : 8 * (4 + p) + 4, :]
    turned = cols[...].T
    lane = lax.broadcasted_iota(jnp.int32, (rows, LANES), 1)
    left, right = slice(0, LANES), slice(width - LANES, width)
    last = LANES - 1
    for p in range(2):
        for c in range(kdev):
            e1[c, p, 0:1, :] = ss[8 * (4 + p) + 4 + c : 8 * (4 + p) + 5 + c, :width]
            e1[c, p, rows - 1 : rows, :] = sn[8 * (4 + p) + 2 + c : 8 * (4 + p) + 3 + c, :width]
            k = 2 * p + c
            e1[c, p, :, left] = jnp.where(lane == 0, rolled(turned[:rows], -k, 1), e1[c, p, :, left])
            k = 4 + 2 * p + c
            e1[c, p, :, right] = jnp.where(lane == last, rolled(turned[:rows], last - k, 1), e1[c, p, :, right])
    for at in range(0, rows, size):
        nxt = min(at + size, rows - 8)
        here = slice(at, at + size)
        _, ax = row_metric(at, size, width, rows)
        md, mn = tile_rows(m, at, size, nxt)
        dd, dn = tile_rows(d, at, size, nxt)
        coef[0, here, :] = (THETA * ax * ax) * (md * east(md) * (dd + east(dd)))
        coef[1, here, :] = (THETA * AY * AY) * (md * mn * (dd + dn))
        for c in range(kdev):
            wt = THETA * ws[c]
            er, ern = tile_rows(e1.at[c, 0], at, size, nxt)
            ei, ein = tile_rows(e1.at[c, 1], at, size, nxt)
            qr, qrn = tile_rows(q.at[c, 0], at, size, nxt)
            qi, qin = tile_rows(q.at[c, 1], at, size, nxt)
            zr, zi = er - qr, ei - qi
            du[c, 0, here, :] = zr - east(zr)
            du[c, 1, here, :] = zi - east(zi)
            dv[c, 0, here, :] = zr - (ern - qrn)
            dv[c, 1, here, :] = zi - (ein - qin)
            base[c, 0, here, :] = md * (er + wt * ei)
            base[c, 1, here, :] = md * (ei - wt * er)


def prepare(e1, q, d, m, ss, sn, sw, se):
    plane = pltpu.VMEM(e1.shape, F32)
    return pl.pallas_call(
        prepare_kernel,
        out_shape=(plane, plane, plane, pltpu.VMEM((2, *d.shape), F32)),
        in_specs=[pl.BlockSpec(memory_space=pltpu.VMEM)] * 8,
        out_specs=[pl.BlockSpec(memory_space=pltpu.VMEM)] * 4,
        scratch_shapes=[pltpu.VMEM(e1.shape, F32), pltpu.VMEM((LANES, sw.shape[1]), F32)],
        compiler_params=PARAMS,
        cost_estimate=pl.CostEstimate(flops=40 * e1.size, bytes_accessed=160 * e1.size, transcendentals=0),
        name="prepare",
    )(*map(vmem, (e1, q, d, m, ss, sn, sw, se)))


def rate(var, d):
    s = var + BACKGROUND
    return (DRAG * (s * lax.rsqrt(s))) * recip(d)


def second_kernel(
    du, dv, base, coef, d, m, mine, other, ss, sn, sw, se, eta_out, fric_out, eta, fric, cols, sems
):
    kdev, _, rows, width = eta.shape
    pad = sw.shape[1]
    size = 16
    ws = omegas(kdev)
    half = rows // 2
    core = lax.rem(lax.axis_index("cons"), 2)
    fric[pl.ds(pl.multiple_of(core * half, 8), half), :] = mine[:half, :]
    fric[pl.ds(pl.multiple_of((1 - core) * half, 8), half), :] = other[:half, :]
    rims = mine[half:, :] + other[half:, :]

    def edge(strip, var_a, var_b):
        zr, zi, dep, ca = (strip[8 * k : 8 * k + 8, :] for k in range(4))
        var = jnp.concatenate([var_a, var_a, var_a, var_a, var_b, var_b, var_b, var_b], axis=0)
        f = rate(var, jnp.maximum(dep, TINY_DEPTH))
        up = lambda x: rolled(x, -2, 0)
        w2 = 2.0 * strip_omega(zr.shape, ws)
        return face(zr, zi, up(zr), up(zi), f + up(f), ca, w2)

    none = jnp.zeros((1, LANES), F32)
    wide = lambda x: jnp.concatenate([x, none], axis=1)
    south = edge(ss, wide(rims[0:1]), wide(rims[1:2]))
    north = edge(sn, wide(rims[2:3]), wide(rims[3:4]))
    west = edge(sw, rims[4:5, :pad], rims[4:5, pad : 2 * pad])
    east_ = edge(se, rims[5:6, :pad], rims[5:6, pad : 2 * pad])

    for p in range(2):
        cols[2 * p : 2 * p + 2, :] = west[p][2:4]
        cols[4 + 2 * p : 6 + 2 * p, :] = east_[p][2:4]
    cols[8:9, :] = rims[4:5, pad : 2 * pad]
    cols[9:10, :] = rims[5:6, :pad]
    turned = cols[...].T

    lane = lax.broadcasted_iota(jnp.int32, (rows, LANES), 1)
    left, right = slice(0, LANES), slice(width - LANES, width)
    last = LANES - 1
    fric[0:1, :] = rims[1:2]
    fric[rows - 1 : rows, :] = rims[2:3]
    fric[:, left] = jnp.where(lane == 0, rolled(turned[:rows], -8, 1), fric[:, left])
    fric[:, right] = jnp.where(lane == last, rolled(turned[:rows], last - 9, 1), fric[:, right])
    for at in range(0, rows, size):
        fric[at : at + size, :] = rate(fric[at : at + size, :], d[at : at + size, :])
    copies = [pltpu.make_async_copy(fric, fric_out, sems.at[0])]
    copies[0].start()

    lane = lax.broadcasted_iota(jnp.int32, (size, LANES), 1)
    last_v = [None] * (2 * kdev)
    for c in range(kdev):
        for p in range(2):
            last_v[2 * c + p] = south[p][2 + c : 3 + c, :width]
    for at in range(0, rows, size):
        nxt = min(at + size, rows - 8)
        here = slice(at, at + size)
        edges = turned[here]
        md = m[here, :]
        rd, rn = tile_rows(fric, at, size, nxt)
        coef_u, coef_v = coef[0, here, :], coef[1, here, :]
        r2u = rd + east(rd)
        r2v = rd + rn
        squ, sqv = r2u * r2u, r2v * r2v

        def with_east(u, k):
            block = jnp.where(lane == last, rolled(edges, last - k, 1), u[:, right])
            return jnp.concatenate([u[:, : width - LANES], block], axis=1)

        def from_west(u, k):
            u = rolled(u, 1, 1)
            block = jnp.where(lane == 0, rolled(edges, -k, 1), u[:, left])
            return jnp.concatenate([block, u[:, LANES:]], axis=1)

        for c in range(kdev):
            w2 = 2.0 * ws[c]
            gu = coef_u * recip(squ + w2 * w2)
            gv = coef_v * recip(sqv + w2 * w2)
            ur, ui = flux(du[c, 0, here, :], du[c, 1, here, :], gu, gu * r2u, w2)
            vr, vi = flux(dv[c, 0, here, :], dv[c, 1, here, :], gv, gv * r2v, w2)
            ur, ui = with_east(ur, 4 + c), with_east(ui, 6 + c)
            if at + size == rows:
                vr = jnp.concatenate([vr[:-1], north[0][2 + c : 3 + c, :width]], axis=0)
                vi = jnp.concatenate([vi[:-1], north[1][2 + c : 3 + c, :width]], axis=0)
            uwr, uwi = from_west(ur, c), from_west(ui, 2 + c)
            vsr = jnp.concatenate([last_v[2 * c], vr[:-1]], axis=0)
            vsi = jnp.concatenate([last_v[2 * c + 1], vi[:-1]], axis=0)
            last_v[2 * c], last_v[2 * c + 1] = vr[-1:], vi[-1:]
            eta[c, 0, here, :] = base[c, 0, here, :] - md * ((ur - uwr) + (vr - vsr))
            eta[c, 1, here, :] = base[c, 1, here, :] - md * ((ui - uwi) + (vi - vsi))
        copies.append(
            pltpu.make_async_copy(eta.at[:, :, here, :], eta_out.at[:, :, here, :], sems.at[len(copies)])
        )
        copies[-1].start()
    for copy in copies:
        copy.wait()


def second_sweep(du, dv, base, coef, d, m, mine, other, ss, sn, sw, se):
    args = (du, dv, base, coef, d, m, mine, other, ss, sn, sw, se)
    return pl.pallas_call(
        second_kernel,
        out_shape=(jax.ShapeDtypeStruct(du.shape, F32), jax.ShapeDtypeStruct(d.shape, F32)),
        in_specs=[pl.BlockSpec(memory_space=pltpu.VMEM)] * len(args),
        out_specs=[pl.BlockSpec(memory_space=pltpu.HBM)] * 2,
        scratch_shapes=[
            pltpu.VMEM(du.shape, F32),
            pltpu.VMEM(d.shape, F32),
            pltpu.VMEM((LANES, sw.shape[1]), F32),
            pltpu.SemaphoreType.DMA((1 + d.shape[0] // 16,)),
        ],
        compiler_params=PARAMS,
        name="second_sweep",
    )(*map(vmem, args))


def swapped(x, axis, bit):
    return lax.ppermute(x, axis, [(i, i ^ bit) for i in range(lax.axis_size(axis))])


def body(elevation, equilibrium, depth, land_mask, friction_prev):
    rows = depth.shape[0]
    ntx, nty, ncons = (lax.axis_size(a) for a in ("tx", "ty", "cons"))
    elev, equil, depth, mask, fric, m2, m1, mn, ms = pack(
        elevation, equilibrium, depth, land_mask, friction_prev
    )
    f2 = lax.ppermute(m2, "tx", [(i, (i - 1 if i % 2 == 0 else i + 1) % ntx) for i in range(ntx)])
    f1 = swapped(m1, "tx", 1)
    e1, send, keep = first_sweep(elev, equil, depth, mask, fric, m1)
    mn, ms, my, send = merge(rows, f1, f2, mn, ms, send)
    recv = swapped(send, "cons", 1)
    if nty == 2:
        fn = fs = swapped(my, "ty", 1)
    else:
        fn = lax.ppermute(ms, "ty", [(i, i - 1) for i in range(1, nty)])
        fs = lax.ppermute(mn, "ty", [(i, i + 1) for i in range(nty - 1)])
    left, right = halves(recv, keep, my)
    ss, sn, sw, se, rims = rim(rows, m1, m2, f1, f2, mn, ms, fn, fs, left)
    prepared = prepare(e1, equil, depth, mask, ss, sn, sw, se)
    parts, bit = [(left, right, rims)], 2
    if bit < ncons:
        parts.append(tuple(swapped(x, "cons", bit) for x in parts[0]))
        bit *= 2
    sums = joined(parts, prepared[2])
    while bit < ncons:
        sums = added(sums, swapped(sums, "cons", bit))
        bit *= 2
    return second_sweep(*prepared, depth, mask, sums, swapped(sums, "cons", 1), ss, sn, sw, se)


def solution(mesh):
    return jax.shard_map(
        body,
        mesh=mesh,
        in_specs=(
            P("cons", None, "ty", "tx"),
            P("cons", None, "ty", "tx"),
            P("ty", "tx"),
            P("ty", "tx"),
            P("ty", "tx"),
        ),
        out_specs=(P("cons", None, "ty", "tx"), P("ty", "tx")),
        check_vma=False,
    )
```

profile of v0, /device:TPU:0, one launch (start us, length us, event | category | flops | bytes accessed | tf_op | source)
XLA Modules:
  0.0 25.0 jit_solution(14699029328945881996)
XLA Ops:
  0.6 2.5 %pack.1 = (f32[2,2,144,512]{3,2,1,0:T(8,128)S(1)}, f32[2,2,144,512]{3,2,1,0:T(8,128)S(1)}, f32[144,512]{1,0:T(8,128)S(1)}, f32[144,512]{1,0:T(8,128)S(1)}, f32[1...) custom-call(f32[2,2,144,512]{3,2,1,0:T(8,128)} %e_in.1, ...), custom_call_target="tpu_custom_call" | custom-call | tf_op jit(solution)/shard_map/pack/pallas_call | solution.py:151
  3.2 5.1 %collective-permute-start = (f32[32,256]{1,0:T(8,128)S(1)}, f32[32,256]{1,0:T(8,128)S(1)}, u32[]{:S(2)}, u32[]{:S(2)}) collective-permute-start(f32[32,256]{1,0:T(8,128)S(1)} %get-tuple-element.36.m2), channel_id=1, source_target_pairs={{0,3},{1,2},{2,1},{3,0},{4,7},{5,6},{6,5},{7,4},{8,11},{9,10},{10,... | collective-permute-start | bytes 98312 | tf_op jit(solution)/shard_map/ppermute | solution.py:633
  8.3 0.0 collective-permute-start.1
  8.3 2.1 %first_sweep.1 = (f32[2,2,144,512]{3,2,1,0:T(8,128)S(1)}, f32[72,512]{1,0:T(8,128)S(1)}, f32[72,512]{1,0:T(8,128)S(1)}) custom-call(f32[2,2,144,512]{3,2,1,0:T(8,128)S(1)} %get-tuple-element.29.e, f32[2,2,144,512]{3,2,1,0:T(8,128)S(1)} %get-tuple-element.30.q, f32[144,512]{1,0:T(8,128)S(1)} %get-tuple-element.31.d, f32[144,512]{1,0:T(8,128)S(1)} %get-tuple-element.32.mask.m, ...), custom_call_target="tpu_custom_call" | custom-call | flops 23592960 | bytes 47185920 | tf_op jit(solution)/shard_map/first_sweep/pallas_call | solution.py:236
  10.4 1.7 %collective-permute-done.1.f1 = f32[24,256]{1,0:T(8,128)S(1)} collective-permute-done((f32[24,256]{1,0:T(8,128)S(1)}, f32[24,256]{1,0:T(8,128)S(1)}, u32[]{:S(2)}, u32[]{:S(2)}) %collective-permute-start.1) | collective-permute-done | bytes 24608 | tf_op jit(solution)/shard_map/ppermute | solution.py:624
  12.1 0.0 collective-permute-done.f2
  12.1 0.1 merge.1
  12.2 0.1 collective-permute-start.2
  12.3 1.6 %collective-permute-start.3 = (f32[32,640]{1,0:T(8,128)S(1)}, f32[32,640]{1,0:T(8,128)S(1)}, u32[]{:S(2)}, u32[]{:S(2)}) collective-permute-start(f32[32,640]{1,0:T(8,128)S(1)} %get-tuple-element.42.after), channel_id=1, source_target_pairs={{0,4},{4,0},{1,5},{5,1},{2,6},{6,2},{3,7},{7,3},{8,12},{12,8},{9,1... | collective-permute-start | bytes 245768 | tf_op jit(solution)/shard_map/ppermute | solution.py:624
  13.8 0.0 collective-permute-done.2.a
  13.9 1.6 %collective-permute-start.4 = (f32[72,256]{1,0:T(8,128)S(1)}, f32[72,256]{1,0:T(8,128)S(1)}, u32[]{:S(2)}, u32[]{:S(2)}) collective-permute-start(f32[72,256]{1,0:T(8,128)S(1)} %get-tuple-element.43.after.refs_0_), channel_id=1, source_target_pairs={{0,16},{8,24},{16,0},{24,8},{1,17},{9,25},{17,1},{25,9},{2,18},{10... | collective-permute-start | bytes 221192 | tf_op jit(solution)/shard_map/ppermute | solution.py:624
  15.5 0.5 %collective-permute-start.5 = (f32[72,256]{1,0:T(8,128)S(1)}, f32[72,256]{1,0:T(8,128)S(1)}, u32[]{:S(2)}, u32[]{:S(2)}) collective-permute-start(f32[72,256]{1,0:T(8,128)S(1)} %get-tuple-element.54.refs_1_), channel_id=1, source_target_pairs={{0,16},{8,24},{16,0},{24,8},{1,17},{9,25},{17,1},{25,9},{2,18},{10... | collective-permute-start | bytes 221192 | tf_op jit(solution)/shard_map/ppermute | solution.py:624
  15.9 1.2 %collective-permute-done.3.fn_ref.fs_ref = f32[32,640]{1,0:T(8,128)S(1)} collective-permute-done((f32[32,640]{1,0:T(8,128)S(1)}, f32[32,640]{1,0:T(8,128)S(1)}, u32[]{:S(2)}, u32[]{:S(2)}) %collective-permute-start.3) | collective-permute-done | bytes 81952 | tf_op jit(solution)/shard_map/ppermute | solution.py:624
  17.1 0.3 %rim.1 = (f32[48,640]{1,0:T(8,128)S(1)}, f32[48,640]{1,0:T(8,128)S(1)}, f32[48,256]{1,0:T(8,128)S(1)}, f32[48,256]{1,0:T(8,128)S(1)}, f32[8,512]{1,0:T(8,128)S(1)}) custom-call(f32[72,256]{1,0:T(8,128)S(1)} %get-tuple-element.43.after.refs_0_, f32[32,256]{1,0:T(8,128)S(1)} %get-tuple-element.36.m2, f32[24,256]{1,0:T(8,128)S(1)} %get-tuple-element.34.after.m1, ...), custom_call_target="tpu_custom_call" | custom-call | tf_op jit(solution)/shard_map/rim/pallas_call | solution.py:437
  17.4 1.6 %collective-permute-start.6 = (f32[8,512]{1,0:T(8,128)S(1)}, f32[8,512]{1,0:T(8,128)S(1)}, u32[]{:S(2)}, u32[]{:S(2)}) collective-permute-start(f32[8,512]{1,0:T(8,128)S(1)} %get-tuple-element.55.refs_2_), channel_id=1, source_target_pairs={{0,16},{8,24},{16,0},{24,8},{1,17},{9,25},{17,1},{25,9},{2,18},{10... | collective-permute-start | bytes 49160 | tf_op jit(solution)/shard_map/ppermute | solution.py:624
  19.0 1.0 %prepare.1 = (f32[2,2,144,512]{3,2,1,0:T(8,128)S(1)}, f32[2,2,144,512]{3,2,1,0:T(8,128)S(1)}, f32[2,2,144,512]{3,2,1,0:T(8,128)S(1)}, f32[2,144,512]{2,1,0:T(8,128)S(1)}) custom-call(f32[2,2,144,512]{3,2,1,0:T(8,128)S(1)} %get-tuple-element.35.e1_in, f32[2,2,144,512]{3,2,1,0:T(8,128)S(1)} %get-tuple-element.30.q, f32[144,512]{1,0:T(8,128)S(1)} %get-tuple-element.31.d, ...), custom_call_target="tpu_custom_call" | custom-call | flops 11796480 | bytes 47185920 | tf_op jit(solution)/shard_map/prepare/pallas_call | solution.py:492
  20.0 1.3 %collective-permute-done.6.refs_5_ = f32[8,512]{1,0:T(8,128)S(1)} collective-permute-done((f32[8,512]{1,0:T(8,128)S(1)}, f32[8,512]{1,0:T(8,128)S(1)}, u32[]{:S(2)}, u32[]{:S(2)}) %collective-permute-start.6) | collective-permute-done | bytes 16416 | tf_op jit(solution)/shard_map/ppermute | solution.py:624
  21.2 0.0 collective-permute-done.4.refs_3_
  21.2 0.0 collective-permute-done.5.refs_4_
  21.2 0.1 collective-permute-start.7
  21.3 1.4 %collective-permute-done.7.other = f32[80,512]{1,0:T(8,128)S(1)} collective-permute-done((f32[80,512]{1,0:T(8,128)S(1)}, f32[80,512]{1,0:T(8,128)S(1)}, u32[]{:S(2)}, u32[]{:S(2)}) %collective-permute-start.7) | collective-permute-done | bytes 163872 | tf_op jit(solution)/shard_map/ppermute | solution.py:624
  22.7 2.3 %second_sweep.1 = (f32[2,2,144,512]{3,2,1,0:T(8,128)}, f32[144,512]{1,0:T(8,128)}) custom-call(f32[2,2,144,512]{3,2,1,0:T(8,128)S(1)} %get-tuple-element.50.du, f32[2,2,144,512]{3,2,1,0:T(8,128)S(1)} %get-tuple-element.51.dv, f32[2,2,144,512]{3,2,1,0:T(8,128)S(1)} %get-tuple-element.52.after.base, f32[2,144,512]{2,1,0:T(8,128)S(1)} %get-tuple-element.53.coef, ...), custom_call_target="tpu_custom_call" | custom-call | tf_op jit(solution)/shard_map/second_sweep/pallas_call | solution.py:607
  (2 shorter events, 0.0 us)
Async XLA Ops:
  3.2 8.9 %collective-permute-start = (f32[32,256]{1,0:T(8,128)S(1)}, f32[32,256]{1,0:T(8,128)S(1)}, u32[]{:S(2)}, u32[]{:S(2)}) collective-permute-start(f32[32,256]{1,0:T(8,128)S(1)} %get-tuple-element.36.m2), channel_id=1, source_target_pairs={{0,3},{1,2},{2,1},{3,0},{4,7},{5,6},{6,5},{7,4},{8,11},{9,10},{10,... | collective-permute-start | bytes 98312 | tf_op jit(solution)/shard_map/ppermute | solution.py:633
  8.3 3.8 %collective-permute-start.1 = (f32[24,256]{1,0:T(8,128)S(1)}, f32[24,256]{1,0:T(8,128)S(1)}, u32[]{:S(2)}, u32[]{:S(2)}) collective-permute-start(f32[24,256]{1,0:T(8,128)S(1)} %get-tuple-element.34.after.m1), channel_id=1, source_target_pairs={{0,1},{1,0},{2,3},{3,2},{4,5},{5,4},{6,7},{7,6},{8,9},{9,8},{10,11... | collective-permute-start | bytes 73736 | tf_op jit(solution)/shard_map/ppermute | solution.py:624
  12.2 1.6 %collective-permute-start.2 = (f32[72,512]{1,0:T(8,128)S(1)}, f32[72,512]{1,0:T(8,128)S(1)}, u32[]{:S(2)}, u32[]{:S(2)}) collective-permute-start(f32[72,512]{1,0:T(8,128)S(1)} %get-tuple-element.40), channel_id=1, source_target_pairs={{0,8},{8,0},{16,24},{24,16},{1,9},{9,1},{17,25},{25,17},{2,10},{10... | collective-permute-start | bytes 442376 | tf_op jit(solution)/shard_map/ppermute | solution.py:624
  12.3 4.9 %collective-permute-start.3 = (f32[32,640]{1,0:T(8,128)S(1)}, f32[32,640]{1,0:T(8,128)S(1)}, u32[]{:S(2)}, u32[]{:S(2)}) collective-permute-start(f32[32,640]{1,0:T(8,128)S(1)} %get-tuple-element.42.after), channel_id=1, source_target_pairs={{0,4},{4,0},{1,5},{5,1},{2,6},{6,2},{3,7},{7,3},{8,12},{12,8},{9,1... | collective-permute-start | bytes 245768 | tf_op jit(solution)/shard_map/ppermute | solution.py:624
  13.9 7.4 %collective-permute-start.4 = (f32[72,256]{1,0:T(8,128)S(1)}, f32[72,256]{1,0:T(8,128)S(1)}, u32[]{:S(2)}, u32[]{:S(2)}) collective-permute-start(f32[72,256]{1,0:T(8,128)S(1)} %get-tuple-element.43.after.refs_0_), channel_id=1, source_target_pairs={{0,16},{8,24},{16,0},{24,8},{1,17},{9,25},{17,1},{25,9},{2,18},{10... | collective-permute-start | bytes 221192 | tf_op jit(solution)/shard_map/ppermute | solution.py:624
  15.5 5.8 %collective-permute-start.5 = (f32[72,256]{1,0:T(8,128)S(1)}, f32[72,256]{1,0:T(8,128)S(1)}, u32[]{:S(2)}, u32[]{:S(2)}) collective-permute-start(f32[72,256]{1,0:T(8,128)S(1)} %get-tuple-element.54.refs_1_), channel_id=1, source_target_pairs={{0,16},{8,24},{16,0},{24,8},{1,17},{9,25},{17,1},{25,9},{2,18},{10... | collective-permute-start | bytes 221192 | tf_op jit(solution)/shard_map/ppermute | solution.py:624
  17.4 3.8 %collective-permute-start.6 = (f32[8,512]{1,0:T(8,128)S(1)}, f32[8,512]{1,0:T(8,128)S(1)}, u32[]{:S(2)}, u32[]{:S(2)}) collective-permute-start(f32[8,512]{1,0:T(8,128)S(1)} %get-tuple-element.55.refs_2_), channel_id=1, source_target_pairs={{0,16},{8,24},{16,0},{24,8},{1,17},{9,25},{17,1},{25,9},{2,18},{10... | collective-permute-start | bytes 49160 | tf_op jit(solution)/shard_map/ppermute | solution.py:624
  21.2 1.5 %collective-permute-start.7 = (f32[80,512]{1,0:T(8,128)S(1)}, f32[80,512]{1,0:T(8,128)S(1)}, u32[]{:S(2)}, u32[]{:S(2)}) collective-permute-start(f32[80,512]{1,0:T(8,128)S(1)} %joined.1.mine), channel_id=1, source_target_pairs={{0,8},{8,0},{16,24},{24,16},{1,9},{9,1},{17,25},{25,17},{2,10},{10... | collective-permute-start | bytes 491528 | tf_op jit(solution)/shard_map/ppermute | solution.py:624
where the time goes:
time: 25.2 us; the launch traced here: 25 us
  starting transfers between devices  10.5 us (42%)
  Pallas kernels  8.3 us (33%)
  waiting for transfers between devices  5.55 us (22%)
  between operations  0.68 us (3%)
    ppermute x7, waiting for transfers between devices, swapped(): lax.ppermute(x, axis, [(i, i ^ bit) for i in range(lax.axis_size(axis))])  5.55 us
    ppermute x7, starting transfers between devices, swapped(): lax.ppermute(x, axis, [(i, i ^ bit) for i in range(lax.axis_size(axis))])  5.38 us
    ppermute x1, starting transfers between devices, body(): lax.ppermute(m2, 'tx', [(i, (i - 1 if i % 2 == 0 else i + 1) % ntx) for i...  5.11 us
    pallas_call x1, Pallas kernels, pack(): pl.pallas_call(pack_kernel, out_shape=(field, field, plane, plane, plane,...  2.52 us
    pallas_call x1, Pallas kernels, second_sweep(): pl.pallas_call(second_kernel, out_shape=(jax.ShapeDtypeStruct(du.shape, F...  2.32 us
    pallas_call x1, Pallas kernels, first_sweep(): pl.pallas_call(first_kernel, out_shape=(pltpu.VMEM(e.shape, F32), half, h...  2.09 us
    pallas_call x1, Pallas kernels, prepare(): pl.pallas_call(prepare_kernel, out_shape=(plane, plane, plane, pltpu.VMEM...  0.97 us
  transfers between devices with their start and end apart: 8, of which 4 were waited for; matrix products, arithmetic and copies ran while one was open for 0% of the time, Pallas kernels for 13%

commit v1 on v0

--- a/solution.py
+++ b/solution.py
@@ -71,7 +71,74 @@
     return a * dr + b * di, a * di - b * dr
 
 
-def pack_kernel(e_in, q_in, d_in, m_in, r_in, e, q, d, m, r, m2, m1, mn, ms, ints, cols, sems):
+def pack_columns_kernel(e_in, q_in, d_in, m_in, r_in, m2, m1, e, q, d, m, r, turned, sems):
+    rows, width = d_in.shape
+    copies = []
+    for s, side in enumerate((slice(0, LANES), slice(width - LANES, width))):
+        for src, dst in ((e_in, e), (q_in, q)):
+            copies.append((src.at[:, :, :, side], dst.at[s]))
+        for src, dst in ((d_in, d), (m_in, m), (r_in, r)):
+            copies.append((src.at[:, side], dst.at[s]))
+    copies = [pltpu.make_async_copy(src, dst, sems.at[k]) for k, (src, dst) in enumerate(copies)]
+    for copy in copies:
+        copy.start()
+    for copy in copies:
+        copy.wait()
+    lane = lax.broadcasted_iota(jnp.int32, (rows, LANES), 1)
+
+    def edges(plane):
+        return jnp.where(lane < LANES // 2, plane(0), plane(1))
+
+    elev = [edges(lambda s: e[s, c, p]) for p in range(2) for c in range(2)]
+    equil = [edges(lambda s: q[s, c, p]) for p in range(2) for c in range(2)]
+    planes = [x - y for x, y in zip(elev, equil)]
+    planes += [edges(lambda s: r[s]), edges(lambda s: d[s]), edges(lambda s: m[s]).astype(F32)]
+    both = jnp.zeros((rows, LANES), F32)
+    for k, plane in enumerate(planes + elev):
+        both = jnp.where((lane >= 4 * k) & (lane < 4 * k + 4), rolled(plane, 4 * k + 2, 1), both)
+    pad = turned.shape[1]
+    turned[...] = jnp.concatenate([both, jnp.zeros((pad - rows, LANES), F32)], axis=0).T
+    odd = lax.rem(lax.axis_index("tx"), 2) == 1
+
+    def put(row, k, east_, west):
+        x, y = turned[4 * k + east_ : 4 * k + east_ + 1, :], turned[4 * k + west : 4 * k + west + 1, :]
+        m1[row : row + 1, :] = jnp.where(odd, y, x)
+        m2[row : row + 1, :] = jnp.where(odd, x, y)
+
+    for g in range(5):
+        for n in range(2):
+            for c in range(2):
+                put(4 * g + 2 * n + c, 2 * g + c if g < 2 else g + 2, n, 2 + n)
+    for c in range(4):
+        put(20 + c, 7 + c, 1, 2)
+    m2[MSG:, :] = jnp.zeros((m2.shape[0] - MSG, pad), F32)
+
+
+def pack_columns(elevation, equilibrium, depth, land_mask, friction):
+    kdev, _, rows, width = elevation.shape
+    pad = -(-rows // LANES) * LANES
+    cut, plane = pltpu.VMEM((2, kdev, 2, rows, LANES), F32), pltpu.VMEM((2, rows, LANES), F32)
+    return pl.pallas_call(
+        pack_columns_kernel,
+        out_shape=(pltpu.VMEM((MSG + 8, pad), F32), pltpu.VMEM((MSG, pad), F32)),
+        in_specs=[pl.BlockSpec(memory_space=pltpu.HBM)] * 5,
+        out_specs=[pl.BlockSpec(memory_space=pltpu.VMEM)] * 2,
+        scratch_shapes=[
+            cut,
+            cut,
+            plane,
+            pltpu.VMEM((2, rows, LANES), jnp.int32),
+            plane,
+            pltpu.VMEM((LANES, pad), F32),
+            pltpu.SemaphoreType.DMA((10,)),
+        ],
+        compiler_params=PARAMS,
+        name="pack_columns",
+    )(*map(hbm, (elevation, equilibrium, depth, land_mask, friction)))
+
+
+def pack_kernel(e_in, q_in, d_in, m_in, r_in, after, e, q, d, m, r, mn, ms, ints, sems):
+    del after
     kdev, _, rows, width = e.shape
     copies = []
 
@@ -91,41 +158,8 @@
     m[...] = ints[...].astype(F32)
     for copy in copies[3:]:
         copy.wait()
-    sides = (slice(0, LANES), slice(width - LANES, width))
+
     ends = (slice(0, 8), slice(rows - 8, rows))
-
-    lane = lax.broadcasted_iota(jnp.int32, (rows, LANES), 1)
-    both = jnp.zeros((rows, LANES), F32)
-    for s in range(2):
-        side = sides[s]
-        planes = [e[c, p, :, side] - q[c, p, :, side] for p in range(2) for c in range(2)]
-        planes += [r[:, side], d[:, side], m[:, side]]
-        planes += [e[c, p, :, side] for p in range(2) for c in range(2)]
-        for k, plane in enumerate(planes):
-            at = 32 * s + 2 * k
-            shift = at if s == 0 else at - (LANES - 2)
-            both = jnp.where((lane == at) | (lane == at + 1), rolled(plane, shift, 1), both)
-    pad = -(-rows // LANES) * LANES
-    turned = jnp.concatenate([both, jnp.zeros((pad - rows, LANES), F32)], axis=0).T
-    for s in range(2):
-        at = 32 * s
-        near = 0 if s == 0 else 1
-        for g in range(2):
-            for line in range(2):
-                for c in range(2):
-                    row = at + 4 * g + 2 * c + line
-                    cols[s, 4 * g + 2 * line + c, :] = turned[row, :]
-        for g in range(2, 5):
-            for line in range(2):
-                for c in range(2):
-                    cols[s, 4 * g + 2 * line + c, :] = turned[at + 2 * (g + 2) + line, :]
-        for c in range(4):
-            cols[s, 20 + c, :] = turned[at + 2 * (7 + c) + near, :]
-    odd = lax.rem(lax.axis_index("tx"), 2)
-    m1[...] = cols[1 - odd]
-    m2[:MSG, :] = cols[odd]
-    m2[MSG:, :] = jnp.zeros((m2.shape[0] - MSG, m2.shape[1]), F32)
-
     for s, out in enumerate((ms, mn)):
         base = 0 if s == 0 else 6
         near = 0 if s == 0 else 7
@@ -143,24 +177,23 @@
                     out[4 * g + 2 * line + c, :width] = plane[base + line, :]
 
 
-def pack(elevation, equilibrium, depth, land_mask, friction):
+def pack(elevation, equilibrium, depth, land_mask, friction, after):
     kdev, _, rows, width = elevation.shape
-    pad = -(-rows // LANES) * LANES
     field, plane = pltpu.VMEM(elevation.shape, F32), pltpu.VMEM(depth.shape, F32)
     row = pltpu.VMEM((MSG, width + LANES), F32)
     return pl.pallas_call(
         pack_kernel,
-        out_shape=(field, field, plane, plane, plane, pltpu.VMEM((MSG + 8, pad), F32), pltpu.VMEM((MSG, pad), F32), row, row),
-        in_specs=[pl.BlockSpec(memory_space=pltpu.HBM)] * 5,
-        out_specs=[pl.BlockSpec(memory_space=pltpu.VMEM)] * 9,
+        out_shape=(field, field, plane, plane, plane, row, row),
+        in_specs=[pl.BlockSpec(memory_space=pltpu.HBM)] * 5 + [pl.BlockSpec(memory_space=pltpu.VMEM)],
+        out_specs=[pl.BlockSpec(memory_space=pltpu.VMEM)] * 7,
         scratch_shapes=[
             pltpu.VMEM(depth.shape, jnp.int32),
-            pltpu.VMEM((2, MSG, pad), F32),
             pltpu.SemaphoreType.DMA((3 + 4 * kdev,)),
         ],
         compiler_params=PARAMS,
+        cost_estimate=pl.CostEstimate(flops=0, bytes_accessed=160 * elevation.size, transcendentals=0),
         name="pack",
-    )(*map(hbm, (elevation, equilibrium, depth, land_mask, friction)))
+    )(*map(hbm, (elevation, equilibrium, depth, land_mask, friction)), vmem(after))
 
 
 def tile_rows(ref, at, size, nxt):
@@ -627,9 +660,9 @@
 def body(elevation, equilibrium, depth, land_mask, friction_prev):
     rows = depth.shape[0]
     ntx, nty, ncons = (lax.axis_size(a) for a in ("tx", "ty", "cons"))
-    elev, equil, depth, mask, fric, m2, m1, mn, ms = pack(
-        elevation, equilibrium, depth, land_mask, friction_prev
-    )
+    fields = (elevation, equilibrium, depth, land_mask, friction_prev)
+    m2, m1 = pack_columns(*fields)
+    elev, equil, depth, mask, fric, mn, ms = pack(*fields, m1)
     f2 = lax.ppermute(m2, "tx", [(i, (i - 1 if i % 2 == 0 else i + 1) % ntx) for i in range(ntx)])
     f1 = swapped(m1, "tx", 1)
     e1, send, keep = first_sweep(elev, equil, depth, mask, fric, m1)

time: 25.2 us -> 24.9 us (0.988)
  waiting for transfers between devices: 5.55 us -> 3.8 us
  Pallas kernels: 8.3 us -> 9.74 us
    pallas_call x0 -> x1, Pallas kernels: none -> 1.85 us  [pack_columns(): pl.pallas_call(pack_columns_kernel, out_shape=(pltpu.VMEM((MSG + 8, pad),...]
    ppermute x7, waiting for transfers between devices: 5.55 us -> 3.79 us  [swapped(): lax.ppermute(x, axis, [(i, i ^ bit) for i in range(lax.axis_size(axis))])]
    pallas_call x1, Pallas kernels: 2.52 us -> 1.99 us  [pack(): pl.pallas_call(pack_kernel, out_shape=(field, field, plane, plane, plane,...]
  transfers between devices with their start and end apart: 8 -> 8, of which waited for: 4 -> 3; matrix products, arithmetic and copies ran while one was open for 0% -> 0% of each run, Pallas kernels for 13% -> 22%
where the time goes in v1:
time: 24.9 us; the launch traced here: 24.7 us
  starting transfers between devices  10.5 us (42%)
  Pallas kernels  9.74 us (39%)
  waiting for transfers between devices  3.8 us (15%)
  between operations  0.7 us (3%)
    ppermute x7, starting transfers between devices, swapped(): lax.ppermute(x, axis, [(i, i ^ bit) for i in range(lax.axis_size(axis))])  5.38 us
    ppermute x1, starting transfers between devices, body(): lax.ppermute(m2, 'tx', [(i, (i - 1 if i % 2 == 0 else i + 1) % ntx) for i...  5.11 us
    ppermute x7, waiting for transfers between devices, swapped(): lax.ppermute(x, axis, [(i, i ^ bit) for i in range(lax.axis_size(axis))])  3.79 us
    pallas_call x1, Pallas kernels, second_sweep(): pl.pallas_call(second_kernel, out_shape=(jax.ShapeDtypeStruct(du.shape, F...  2.32 us
    pallas_call x1, Pallas kernels, first_sweep(): pl.pallas_call(first_kernel, out_shape=(pltpu.VMEM(e.shape, F32), half, h...  2.17 us
    pallas_call x1, Pallas kernels, pack(): pl.pallas_call(pack_kernel, out_shape=(field, field, plane, plane, plane,...  1.99 us
    pallas_call x1, Pallas kernels, pack_columns(): pl.pallas_call(pack_columns_kernel, out_shape=(pltpu.VMEM((MSG + 8, pad),...  1.85 us
    pallas_call x1, Pallas kernels, prepare(): pl.pallas_call(prepare_kernel, out_shape=(plane, plane, plane, pltpu.VMEM...  1 us
  transfers between devices with their start and end apart: 8, of which 3 were waited for; matrix products, arithmetic and copies ran while one was open for 0% of the time, Pallas kernels for 22%

profile of v1, /device:TPU:0, one launch (start us, length us, event | category | flops | bytes accessed | tf_op | source)
XLA Modules:
  0.0 24.7 jit_solution(9269789605397907491)
XLA Ops:
  0.6 1.9 %pack_columns.1 = (f32[32,256]{1,0:T(8,128)S(1)}, f32[24,256]{1,0:T(8,128)S(1)}) custom-call(f32[2,2,144,512]{3,2,1,0:T(8,128)} %e_in.3, f32[2,2,144,512]{3,2,1,0:T(8,128)} %q_in.3, f32[144,512]{1,0:T(8,128)} %d_in.3, s32[144,512]{1,0:T(8,128)} %m_in.3, f32[144,512]{1,0:T(8,128)} %r_in.3), custom_call_target="tpu_custom_call" | custom-call | tf_op jit(solution)/shard_map/pack_columns/pallas_call | solution.py:121
  2.5 5.1 %collective-permute-start = (f32[32,256]{1,0:T(8,128)S(1)}, f32[32,256]{1,0:T(8,128)S(1)}, u32[]{:S(2)}, u32[]{:S(2)}) collective-permute-start(f32[32,256]{1,0:T(8,128)S(1)} %get-tuple-element.36.m2), channel_id=1, source_target_pairs={{0,3},{1,2},{2,1},{3,0},{4,7},{5,6},{6,5},{7,4},{8,11},{9,10},{10,... | collective-permute-start | bytes 98312 | tf_op jit(solution)/shard_map/ppermute | solution.py:666
  7.6 0.0 collective-permute-start.1
  7.6 2.0 %pack.1 = (f32[2,2,144,512]{3,2,1,0:T(8,128)S(1)}, f32[2,2,144,512]{3,2,1,0:T(8,128)S(1)}, f32[144,512]{1,0:T(8,128)S(1)}, f32[144,512]{1,0:T(8,128)S(1)}, f32[1...) custom-call(f32[2,2,144,512]{3,2,1,0:T(8,128)} %e_in.3, f32[2,2,144,512]{3,2,1,0:T(8,128)} %q_in.3, ...), custom_call_target="tpu_custom_call" | custom-call | bytes 47185920 | tf_op jit(solution)/shard_map/pack/pallas_call | solution.py:184
  9.6 2.2 %first_sweep.1 = (f32[2,2,144,512]{3,2,1,0:T(8,128)S(1)}, f32[72,512]{1,0:T(8,128)S(1)}, f32[72,512]{1,0:T(8,128)S(1)}) custom-call(f32[2,2,144,512]{3,2,1,0:T(8,128)S(1)} %get-tuple-element.30.e, f32[2,2,144,512]{3,2,1,0:T(8,128)S(1)} %get-tuple-element.31.q, f32[144,512]{1,0:T(8,128)S(1)} %get-tuple-element.32.d, f32[144,512]{1,0:T(8,128)S(1)} %get-tuple-element.33.mask.m, ...), custom_call_target="tpu_custom_call" | custom-call | flops 23592960 | bytes 47185920 | tf_op jit(solution)/shard_map/first_sweep/pallas_call | solution.py:269
  11.8 0.0 collective-permute-done.1.f1
  11.8 0.0 collective-permute-done.f2
  11.8 0.1 merge.1
  11.9 0.1 collective-permute-start.2
  12.0 1.6 %collective-permute-start.3 = (f32[32,640]{1,0:T(8,128)S(1)}, f32[32,640]{1,0:T(8,128)S(1)}, u32[]{:S(2)}, u32[]{:S(2)}) collective-permute-start(f32[32,640]{1,0:T(8,128)S(1)} %get-tuple-element.42.after), channel_id=1, source_target_pairs={{0,4},{4,0},{1,5},{5,1},{2,6},{6,2},{3,7},{7,3},{8,12},{12,8},{9,1... | collective-permute-start | bytes 245768 | tf_op jit(solution)/shard_map/ppermute | solution.py:657
  13.5 0.0 collective-permute-done.2.a
  13.6 1.6 %collective-permute-start.4 = (f32[72,256]{1,0:T(8,128)S(1)}, f32[72,256]{1,0:T(8,128)S(1)}, u32[]{:S(2)}, u32[]{:S(2)}) collective-permute-start(f32[72,256]{1,0:T(8,128)S(1)} %get-tuple-element.43.after.refs_0_), channel_id=1, source_target_pairs={{0,16},{8,24},{16,0},{24,8},{1,17},{9,25},{17,1},{25,9},{2,18},{10... | collective-permute-start | bytes 221192 | tf_op jit(solution)/shard_map/ppermute | solution.py:657
  15.2 0.5 %collective-permute-start.5 = (f32[72,256]{1,0:T(8,128)S(1)}, f32[72,256]{1,0:T(8,128)S(1)}, u32[]{:S(2)}, u32[]{:S(2)}) collective-permute-start(f32[72,256]{1,0:T(8,128)S(1)} %get-tuple-element.54.refs_1_), channel_id=1, source_target_pairs={{0,16},{8,24},{16,0},{24,8},{1,17},{9,25},{17,1},{25,9},{2,18},{10... | collective-permute-start | bytes 221192 | tf_op jit(solution)/shard_map/ppermute | solution.py:657
  15.6 1.2 %collective-permute-done.3.fn_ref.fs_ref = f32[32,640]{1,0:T(8,128)S(1)} collective-permute-done((f32[32,640]{1,0:T(8,128)S(1)}, f32[32,640]{1,0:T(8,128)S(1)}, u32[]{:S(2)}, u32[]{:S(2)}) %collective-permute-start.3) | collective-permute-done | bytes 81952 | tf_op jit(solution)/shard_map/ppermute | solution.py:657
  16.8 0.3 %rim.1 = (f32[48,640]{1,0:T(8,128)S(1)}, f32[48,640]{1,0:T(8,128)S(1)}, f32[48,256]{1,0:T(8,128)S(1)}, f32[48,256]{1,0:T(8,128)S(1)}, f32[8,512]{1,0:T(8,128)S(1)}) custom-call(f32[72,256]{1,0:T(8,128)S(1)} %get-tuple-element.43.after.refs_0_, f32[32,256]{1,0:T(8,128)S(1)} %get-tuple-element.36.m2, f32[24,256]{1,0:T(8,128)S(1)} %get-tuple-element.29.after.m1, ...), custom_call_target="tpu_custom_call" | custom-call | tf_op jit(solution)/shard_map/rim/pallas_call | solution.py:470
  17.1 1.6 %collective-permute-start.6 = (f32[8,512]{1,0:T(8,128)S(1)}, f32[8,512]{1,0:T(8,128)S(1)}, u32[]{:S(2)}, u32[]{:S(2)}) collective-permute-start(f32[8,512]{1,0:T(8,128)S(1)} %get-tuple-element.55.refs_2_), channel_id=1, source_target_pairs={{0,16},{8,24},{16,0},{24,8},{1,17},{9,25},{17,1},{25,9},{2,18},{10... | collective-permute-start | bytes 49160 | tf_op jit(solution)/shard_map/ppermute | solution.py:657
  18.7 1.0 %prepare.1 = (f32[2,2,144,512]{3,2,1,0:T(8,128)S(1)}, f32[2,2,144,512]{3,2,1,0:T(8,128)S(1)}, f32[2,2,144,512]{3,2,1,0:T(8,128)S(1)}, f32[2,144,512]{2,1,0:T(8,128)S(1)}) custom-call(f32[2,2,144,512]{3,2,1,0:T(8,128)S(1)} %get-tuple-element.35.e1_in, f32[2,2,144,512]{3,2,1,0:T(8,128)S(1)} %get-tuple-element.31.q, f32[144,512]{1,0:T(8,128)S(1)} %get-tuple-element.32.d, ...), custom_call_target="tpu_custom_call" | custom-call | flops 11796480 | bytes 47185920 | tf_op jit(solution)/shard_map/prepare/pallas_call | solution.py:525
  19.7 1.2 %collective-permute-done.6.refs_5_ = f32[8,512]{1,0:T(8,128)S(1)} collective-permute-done((f32[8,512]{1,0:T(8,128)S(1)}, f32[8,512]{1,0:T(8,128)S(1)}, u32[]{:S(2)}, u32[]{:S(2)}) %collective-permute-start.6) | collective-permute-done | bytes 16416 | tf_op jit(solution)/shard_map/ppermute | solution.py:657
  20.9 0.0 collective-permute-done.4.refs_3_
  20.9 0.0 collective-permute-done.5.refs_4_
  20.9 0.1 collective-permute-start.7
  21.0 1.4 %collective-permute-done.7.other = f32[80,512]{1,0:T(8,128)S(1)} collective-permute-done((f32[80,512]{1,0:T(8,128)S(1)}, f32[80,512]{1,0:T(8,128)S(1)}, u32[]{:S(2)}, u32[]{:S(2)}) %collective-permute-start.7) | collective-permute-done | bytes 163872 | tf_op jit(solution)/shard_map/ppermute | solution.py:657
  22.4 2.3 %second_sweep.1 = (f32[2,2,144,512]{3,2,1,0:T(8,128)}, f32[144,512]{1,0:T(8,128)}) custom-call(f32[2,2,144,512]{3,2,1,0:T(8,128)S(1)} %get-tuple-element.50.du, f32[2,2,144,512]{3,2,1,0:T(8,128)S(1)} %get-tuple-element.51.dv, f32[2,2,144,512]{3,2,1,0:T(8,128)S(1)} %get-tuple-element.52.after.base, f32[2,144,512]{2,1,0:T(8,128)S(1)} %get-tuple-element.53.coef, ...), custom_call_target="tpu_custom_call" | custom-call | tf_op jit(solution)/shard_map/second_sweep/pallas_call | solution.py:640
  (2 shorter events, 0.0 us)
Async XLA Ops:
  2.5 9.3 %collective-permute-start = (f32[32,256]{1,0:T(8,128)S(1)}, f32[32,256]{1,0:T(8,128)S(1)}, u32[]{:S(2)}, u32[]{:S(2)}) collective-permute-start(f32[32,256]{1,0:T(8,128)S(1)} %get-tuple-element.36.m2), channel_id=1, source_target_pairs={{0,3},{1,2},{2,1},{3,0},{4,7},{5,6},{6,5},{7,4},{8,11},{9,10},{10,... | collective-permute-start | bytes 98312 | tf_op jit(solution)/shard_map/ppermute | solution.py:666
  7.6 4.2 %collective-permute-start.1 = (f32[24,256]{1,0:T(8,128)S(1)}, f32[24,256]{1,0:T(8,128)S(1)}, u32[]{:S(2)}, u32[]{:S(2)}) collective-permute-start(f32[24,256]{1,0:T(8,128)S(1)} %get-tuple-element.29.after.m1), channel_id=1, source_target_pairs={{0,1},{1,0},{2,3},{3,2},{4,5},{5,4},{6,7},{7,6},{8,9},{9,8},{10,11... | collective-permute-start | bytes 73736 | tf_op jit(solution)/shard_map/ppermute | solution.py:657
  11.9 1.6 %collective-permute-start.2 = (f32[72,512]{1,0:T(8,128)S(1)}, f32[72,512]{1,0:T(8,128)S(1)}, u32[]{:S(2)}, u32[]{:S(2)}) collective-permute-start(f32[72,512]{1,0:T(8,128)S(1)} %get-tuple-element.40), channel_id=1, source_target_pairs={{0,8},{8,0},{16,24},{24,16},{1,9},{9,1},{17,25},{25,17},{2,10},{10... | collective-permute-start | bytes 442376 | tf_op jit(solution)/shard_map/ppermute | solution.py:657
  12.0 4.9 %collective-permute-start.3 = (f32[32,640]{1,0:T(8,128)S(1)}, f32[32,640]{1,0:T(8,128)S(1)}, u32[]{:S(2)}, u32[]{:S(2)}) collective-permute-start(f32[32,640]{1,0:T(8,128)S(1)} %get-tuple-element.42.after), channel_id=1, source_target_pairs={{0,4},{4,0},{1,5},{5,1},{2,6},{6,2},{3,7},{7,3},{8,12},{12,8},{9,1... | collective-permute-start | bytes 245768 | tf_op jit(solution)/shard_map/ppermute | solution.py:657
  13.6 7.4 %collective-permute-start.4 = (f32[72,256]{1,0:T(8,128)S(1)}, f32[72,256]{1,0:T(8,128)S(1)}, u32[]{:S(2)}, u32[]{:S(2)}) collective-permute-start(f32[72,256]{1,0:T(8,128)S(1)} %get-tuple-element.43.after.refs_0_), channel_id=1, source_target_pairs={{0,16},{8,24},{16,0},{24,8},{1,17},{9,25},{17,1},{25,9},{2,18},{10... | collective-permute-start | bytes 221192 | tf_op jit(solution)/shard_map/ppermute | solution.py:657
  15.2 5.8 %collective-permute-start.5 = (f32[72,256]{1,0:T(8,128)S(1)}, f32[72,256]{1,0:T(8,128)S(1)}, u32[]{:S(2)}, u32[]{:S(2)}) collective-permute-start(f32[72,256]{1,0:T(8,128)S(1)} %get-tuple-element.54.refs_1_), channel_id=1, source_target_pairs={{0,16},{8,24},{16,0},{24,8},{1,17},{9,25},{17,1},{25,9},{2,18},{10... | collective-permute-start | bytes 221192 | tf_op jit(solution)/shard_map/ppermute | solution.py:657
  17.1 3.8 %collective-permute-start.6 = (f32[8,512]{1,0:T(8,128)S(1)}, f32[8,512]{1,0:T(8,128)S(1)}, u32[]{:S(2)}, u32[]{:S(2)}) collective-permute-start(f32[8,512]{1,0:T(8,128)S(1)} %get-tuple-element.55.refs_2_), channel_id=1, source_target_pairs={{0,16},{8,24},{16,0},{24,8},{1,17},{9,25},{17,1},{25,9},{2,18},{10... | collective-permute-start | bytes 49160 | tf_op jit(solution)/shard_map/ppermute | solution.py:657
  20.9 1.5 %collective-permute-start.7 = (f32[80,512]{1,0:T(8,128)S(1)}, f32[80,512]{1,0:T(8,128)S(1)}, u32[]{:S(2)}, u32[]{:S(2)}) collective-permute-start(f32[80,512]{1,0:T(8,128)S(1)} %joined.1.mine), channel_id=1, source_target_pairs={{0,8},{8,0},{16,24},{24,16},{1,9},{9,1},{17,25},{25,17},{2,10},{10... | collective-permute-start | bytes 491528 | tf_op jit(solution)/shard_map/ppermute | solution.py:657

commit v2 on v1

--- a/solution.py
+++ b/solution.py
@@ -15,8 +15,7 @@
 BACKGROUND = 0.01
 F32 = jnp.float32
 LANES = 128
-FIELDS = 6
-MSG = 4 * FIELDS
+MSG = 16
 TINY_DEPTH = 1e-6
 PARAMS = pltpu.CompilerParams(vmem_limit_bytes=16 * 1024 * 1024)
 
@@ -99,19 +98,32 @@
     pad = turned.shape[1]
     turned[...] = jnp.concatenate([both, jnp.zeros((pad - rows, LANES), F32)], axis=0).T
     odd = lax.rem(lax.axis_index("tx"), 2) == 1
-
-    def put(row, k, east_, west):
-        x, y = turned[4 * k + east_ : 4 * k + east_ + 1, :], turned[4 * k + west : 4 * k + west + 1, :]
-        m1[row : row + 1, :] = jnp.where(odd, y, x)
-        m2[row : row + 1, :] = jnp.where(odd, x, y)
-
-    for g in range(5):
-        for n in range(2):
-            for c in range(2):
-                put(4 * g + 2 * n + c, 2 * g + c if g < 2 else g + 2, n, 2 + n)
-    for c in range(4):
-        put(20 + c, 7 + c, 1, 2)
-    m2[MSG:, :] = jnp.zeros((m2.shape[0] - MSG, pad), F32)
+    first = (lax.axis_index("ty") * rows).astype(F32)
+    lat_row = jnp.minimum(lax.broadcasted_iota(jnp.int32, (1, pad), 1), rows).astype(F32) + first
+    ax = metric(lat_row, rows * lax.axis_size("ty"))
+    ws = omegas(2)
+
+    def line(k, at):
+        return turned[4 * k + at : 4 * k + at + 1, :]
+
+    def message(near, far):
+        low, high = min(near, far), max(near, far)
+        coef = (THETA * ax * ax) * (line(6, low) * line(6, high) * (line(5, low) + line(5, high)))
+        r2 = line(4, low) + line(4, high)
+        behind = []
+        for c in range(2):
+            behind.append(
+                face(line(c, low), line(2 + c, low), line(c, high), line(2 + c, high), r2, coef, 2.0 * ws[c])
+            )
+        out = [line(k, near) for k in range(4)]
+        out += [behind[c][p] for p in range(2) for c in range(2)]
+        return out + [line(k, near) for k in (7, 8, 9, 10, 4, 5, 6)]
+
+    for k, (x, y) in enumerate(zip(message(1, 0), message(2, 3))):
+        m1[k : k + 1, :] = jnp.where(odd, y, x)
+        m2[k : k + 1, :] = jnp.where(odd, x, y)[:, :rows]
+    m1[MSG - 1 :, :] = jnp.zeros((1, pad), F32)
+    m2[MSG - 1 :, :] = jnp.zeros((1, rows), F32)
 
 
 def pack_columns(elevation, equilibrium, depth, land_mask, friction):
@@ -120,7 +132,7 @@
     cut, plane = pltpu.VMEM((2, kdev, 2, rows, LANES), F32), pltpu.VMEM((2, rows, LANES), F32)
     return pl.pallas_call(
         pack_columns_kernel,
-        out_shape=(pltpu.VMEM((MSG + 8, pad), F32), pltpu.VMEM((MSG, pad), F32)),
+        out_shape=(pltpu.VMEM((MSG, rows), F32), pltpu.VMEM((MSG, pad), F32)),
         in_specs=[pl.BlockSpec(memory_space=pltpu.HBM)] * 5,
         out_specs=[pl.BlockSpec(memory_space=pltpu.VMEM)] * 2,
         scratch_shapes=[
@@ -137,63 +149,42 @@
     )(*map(hbm, (elevation, equilibrium, depth, land_mask, friction)))
 
 
-def pack_kernel(e_in, q_in, d_in, m_in, r_in, after, e, q, d, m, r, mn, ms, ints, sems):
+def pack_kernel(e, q, d, ints, r, after, m, mn, ms):
     del after
     kdev, _, rows, width = e.shape
-    copies = []
-
-    def fetch(src, dst):
-        copy = pltpu.make_async_copy(src, dst, sems.at[len(copies)])
-        copy.start()
-        copies.append(copy)
-
-    for src, dst in ((d_in, d), (m_in, ints), (r_in, r)):
-        fetch(src, dst)
-    for c in range(kdev):
-        for p in range(2):
-            fetch(e_in.at[c, p], e.at[c, p])
-            fetch(q_in.at[c, p], q.at[c, p])
-    for copy in copies[:3]:
-        copy.wait()
     m[...] = ints[...].astype(F32)
-    for copy in copies[3:]:
-        copy.wait()
-
-    ends = (slice(0, 8), slice(rows - 8, rows))
-    for s, out in enumerate((ms, mn)):
-        base = 0 if s == 0 else 6
-        near = 0 if s == 0 else 7
+    ws = omegas(kdev)
+    for out, end, near, low in ((ms, slice(0, 8), 0, 0), (mn, slice(rows - 8, rows), 7, 6)):
         out[:, width:] = jnp.zeros((MSG, LANES), F32)
-        for p in range(2):
-            for c in range(2):
-                line8 = e[c, p, ends[s], :]
-                z = line8 - q[c, p, ends[s], :]
-                for line in range(2):
-                    out[4 * p + 2 * line + c, :width] = z[base + line, :]
-                out[20 + 2 * p + c, :width] = line8[near, :]
-        for g, plane in ((2, r[ends[s], :]), (3, d[ends[s], :]), (4, m[ends[s], :])):
-            for line in range(2):
-                for c in range(2):
-                    out[4 * g + 2 * line + c, :width] = plane[base + line, :]
+        r8, d8, m8 = r[end, :], d[end, :], m[end, :]
+        up = lambda x: rolled(x, -1, 0)
+        coef = (THETA * AY * AY) * (m8 * up(m8) * (d8 + up(d8)))
+        r2 = r8 + up(r8)
+        for c in range(kdev):
+            elev = [e[c, p, end, :] for p in range(2)]
+            z = [elev[p] - q[c, p, end, :] for p in range(2)]
+            v = face(z[0], z[1], up(z[0]), up(z[1]), r2, coef, 2.0 * ws[c])
+            for p in range(2):
+                out[2 * p + c, :width] = z[p][near, :]
+                out[4 + 2 * p + c, :width] = v[p][low, :]
+                out[8 + 2 * p + c, :width] = elev[p][near, :]
+        for k, plane in enumerate((r8, d8, m8)):
+            out[12 + k, :width] = plane[near, :]
+        out[MSG - 1, :width] = jnp.zeros((width,), F32)
 
 
 def pack(elevation, equilibrium, depth, land_mask, friction, after):
     kdev, _, rows, width = elevation.shape
-    field, plane = pltpu.VMEM(elevation.shape, F32), pltpu.VMEM(depth.shape, F32)
+    plane = pltpu.VMEM(depth.shape, F32)
     row = pltpu.VMEM((MSG, width + LANES), F32)
     return pl.pallas_call(
         pack_kernel,
-        out_shape=(field, field, plane, plane, plane, row, row),
-        in_specs=[pl.BlockSpec(memory_space=pltpu.HBM)] * 5 + [pl.BlockSpec(memory_space=pltpu.VMEM)],
-        out_specs=[pl.BlockSpec(memory_space=pltpu.VMEM)] * 7,
-        scratch_shapes=[
-            pltpu.VMEM(depth.shape, jnp.int32),
-            pltpu.SemaphoreType.DMA((3 + 4 * kdev,)),
-        ],
-        compiler_params=PARAMS,
-        cost_estimate=pl.CostEstimate(flops=0, bytes_accessed=160 * elevation.size, transcendentals=0),
+        out_shape=(plane, row, row),
+        in_specs=[pl.BlockSpec(memory_space=pltpu.VMEM)] * 6,
+        out_specs=[pl.BlockSpec(memory_space=pltpu.VMEM)] * 3,
+        compiler_params=PARAMS,
         name="pack",
-    )(*map(hbm, (elevation, equilibrium, depth, land_mask, friction)), vmem(after))
+    )(*map(vmem, (elevation, equilibrium, depth, land_mask, friction, after)))
 
 
 def tile_rows(ref, at, size, nxt):
@@ -293,45 +284,57 @@
     )(vmem(a), vmem(b), *map(vmem, after))
 
 
-def halves_kernel(a, b, after, left, right):
+def cut_kernel(a, b, after, *outs):
     del after
-    cut = left.shape[1]
-    left[...] = a[:, :cut] + b[:, :cut]
-    right[...] = a[:, cut:] + b[:, cut:]
-
-
-def halves(a, b, after):
-    part = pltpu.VMEM((a.shape[0], a.shape[1] // 2), F32)
-    return pl.pallas_call(
-        halves_kernel,
-        out_shape=(part, part),
+    at = 0
+    for out in outs:
+        here = slice(at, at + out.shape[0])
+        out[...] = a[here, :] + b[here, :]
+        at += out.shape[0]
+
+
+def cut_sum(a, b, after):
+    rows, width = a.shape
+    large = pltpu.VMEM(((rows - 8) // 2, width), F32)
+    return pl.pallas_call(
+        cut_kernel,
+        out_shape=(large, large, pltpu.VMEM((8, width), F32)),
         in_specs=[pl.BlockSpec(memory_space=pltpu.VMEM)] * 3,
-        out_specs=[pl.BlockSpec(memory_space=pltpu.VMEM)] * 2,
-        compiler_params=PARAMS,
-        name="halves",
+        out_specs=[pl.BlockSpec(memory_space=pltpu.VMEM)] * 3,
+        compiler_params=PARAMS,
+        name="cut_sum",
     )(vmem(a), vmem(b), vmem(after))
+
+
+def tree_sum(terms):
+    while len(terms) > 1:
+        terms = [a + b for a, b in zip(terms[::2], terms[1::2])]
+    return terms[0]
 
 
 def join_kernel(after, *refs):
     del after
-    out = refs[-1]
-    rows, cut = refs[0].shape
-    for k, at in enumerate((slice(0, cut), slice(cut, 2 * cut))):
-        out[:rows, at] = functools.reduce(jnp.add, [ref[...] for ref in refs[k:-1:3]])
-    out[rows:, :] = functools.reduce(jnp.add, [ref[...] for ref in refs[2:-1:3]])
-
-
-def joined(parts, after):
-    (rows, cut), rims = parts[0][0].shape, parts[0][2].shape[0]
-    flat = [x for part in parts for x in part]
+    mine, rims = refs[-2:]
+    pieces, partner, others = refs[:3], refs[3:6], refs[6:-2]
+    large = pieces[0].shape[0]
+    mine[:large, :] = pieces[0][...] + partner[0][...]
+    mine[large : 2 * large, :] = pieces[1][...] + partner[1][...]
+    mine[2 * large :, :] = pieces[2][:8, :] + partner[2][:8, :]
+    terms = [x[...] for x in others]
+    rims[...] = tree_sum([pieces[2][8:, :], terms[0], partner[2][8:, :], *terms[1:]])
+
+
+def joined(pieces, partner, others, after):
+    width = pieces[0].shape[1]
+    args = (after, *pieces, *partner, *others)
     return pl.pallas_call(
         join_kernel,
-        out_shape=pltpu.VMEM((rows + rims, 2 * cut), F32),
-        in_specs=[pl.BlockSpec(memory_space=pltpu.VMEM)] * (1 + len(flat)),
-        out_specs=pl.BlockSpec(memory_space=pltpu.VMEM),
+        out_shape=(pltpu.VMEM((2 * pieces[0].shape[0] + 8, width), F32), pltpu.VMEM((8, width), F32)),
+        in_specs=[pl.BlockSpec(memory_space=pltpu.VMEM)] * len(args),
+        out_specs=[pl.BlockSpec(memory_space=pltpu.VMEM)] * 2,
         compiler_params=PARAMS,
         name="joined",
-    )(*map(vmem, (after, *flat)))
+    )(*map(vmem, args))
 
 
 def roles(a, b):
@@ -339,25 +342,27 @@
     return jnp.where(even, b, a), jnp.where(even, a, b)
 
 
+def padded(x, pad):
+    return jnp.concatenate([x, jnp.zeros((x.shape[0], pad - x.shape[1]), F32)], axis=1)
+
+
 def merge_kernel(rows, f2, f1, mn, ms, send, mn_out, ms_out, my_out, send_out):
     width = mn.shape[1] - LANES
-    fw, fe = roles(f1[...], f2[:MSG, :])
-    block = (rows - 1) // LANES * LANES
+    fw, fe = roles(f1[...], padded(f2[...], f1.shape[1]))
     lane = lax.broadcasted_iota(jnp.int32, (MSG, LANES), 1)
-    in_block = rows - 1 - block
-    fe_last = rolled(rolled(fe[:, block : block + LANES], -in_block, 1), 2, 0)
-    fw_last = rolled(fw[:, block : block + LANES], LANES - 1 - in_block, 1)
-    fe_first = fe[:, :LANES]
-    fw_first = rolled(rolled(fw[:, :LANES], LANES - 1, 1), -2, 0)
-    n_end = jnp.where(lane == 0, fe_last, jnp.where(lane == LANES - 1, fw_last, 0.0))
-    s_end = jnp.where(lane == 0, fe_first, jnp.where(lane == LANES - 1, fw_first, 0.0))
+    last = LANES - 1
+
+    def ends(at):
+        east_, west = fe[:, at // LANES * LANES :][:, :LANES], fw[:, at // LANES * LANES :][:, :LANES]
+        east_, west = rolled(east_, -(at % LANES), 1), rolled(west, last - at % LANES, 1)
+        return jnp.where(lane == 0, east_, jnp.where(lane == last, west, 0.0))
+
     mn_out[:, :width] = mn[:, :width]
     ms_out[:, :width] = ms[:, :width]
-    mn_out[:, width:] = n_end
-    ms_out[:, width:] = s_end
+    mn_out[:, width:] = ends(rows - 1)
+    ms_out[:, width:] = ends(0)
     low = lax.axis_index("ty") == 0
-    my_out[:MSG, :] = jnp.where(low, mn_out[...], ms_out[...])
-    my_out[MSG:, :] = jnp.zeros((my_out.shape[0] - MSG, my_out.shape[1]), F32)
+    my_out[...] = jnp.where(low, mn_out[...], ms_out[...])
     send_out[...] = send[...]
 
 
@@ -365,7 +370,7 @@
     out = pltpu.VMEM(mn.shape, F32)
     return pl.pallas_call(
         functools.partial(merge_kernel, rows),
-        out_shape=(out, out, pltpu.VMEM((MSG + 8, mn.shape[1]), F32), pltpu.VMEM(send.shape, F32)),
+        out_shape=(out, out, out, pltpu.VMEM(send.shape, F32)),
         in_specs=[pl.BlockSpec(memory_space=pltpu.VMEM)] * 5,
         out_specs=[pl.BlockSpec(memory_space=pltpu.VMEM)] * 4,
         compiler_params=PARAMS,
@@ -379,11 +384,20 @@
 
 
 def strip_sweep(low, high, ws, g_across, g_along):
-    field = [jnp.concatenate([low[4 * g : 4 * g + 4], high[4 * g : 4 * g + 4]], axis=0) for g in range(5)]
-    zr, zi, r, d, m = field
     none = jnp.zeros((2, low.shape[1]), F32)
-    er = jnp.concatenate([none, low[20:22], high[20:22], none], axis=0)
-    ei = jnp.concatenate([none, low[22:24], high[22:24], none], axis=0)
+
+    def field(at):
+        return jnp.concatenate([none, low[at : at + 2], high[at : at + 2], none], axis=0)
+
+    def single(at):
+        a, b = low[at : at + 1], high[at : at + 1]
+        return jnp.concatenate([none, a, a, b, b, none], axis=0)
+
+    def given(at):
+        return jnp.concatenate([low[at : at + 2], none, high[at : at + 2], none], axis=0)
+
+    zr, zi, er, ei = field(0), field(2), field(8), field(10)
+    r, d, m = single(12), single(13), single(14)
     w = strip_omega(zr.shape, ws)
     w2 = 2.0 * w
     wt = THETA * w
@@ -392,6 +406,8 @@
     coef_a = (THETA * g_across * g_across) * (m * up(m) * (d + up(d)))
     coef_l = (THETA * g_along * g_along) * (m * nx(m) * (d + nx(d)))
     ar, ai = face(zr, zi, up(zr), up(zi), r + up(r), coef_a, w2)
+    middle = lax.broadcasted_iota(jnp.int32, zr.shape, 0) // 2 == 1
+    ar, ai = jnp.where(middle, ar, given(4)), jnp.where(middle, ai, given(6))
     lr, li = face(zr, zi, nx(zr), nx(zi), r + nx(r), coef_l, w2)
     abr, abi = rolled(ar, 2, 0), rolled(ai, 2, 0)
     lbr, lbi = rolled(lr, 1, 1), rolled(li, 1, 1)
@@ -409,7 +425,7 @@
     return (z1r, z1i, d, coef_a, e1r, e1i), var
 
 
-def rim_kernel(rows, after, m2, m1, f2, f1, mn, ms, fn_ref, fs_ref, s_out, n_out, w_out, e_out, sums):
+def rim_kernel(rows, late, m2, m1, f2, f1, mn, ms, fn_ref, fs_ref, s_out, n_out, w_out, e_out, sums, tail):
     kdev = 2
     width = mn.shape[1] - LANES
     pad = m1.shape[1]
@@ -417,8 +433,8 @@
     ty, count = lax.axis_index("ty"), lax.axis_size("ty")
     first = (ty * rows).astype(F32)
     total = rows * count
-    fn = jnp.where(ty < count - 1, fn_ref[:MSG, :], 0.0)
-    fs = jnp.where(ty > 0, fs_ref[:MSG, :], 0.0)
+    fn = jnp.where(ty < count - 1, fn_ref[...], 0.0)
+    fs = jnp.where(ty > 0, fs_ref[...], 0.0)
 
     ay = AY
     line = lax.broadcasted_iota(jnp.int32, (8, LANES), 0) // 2
@@ -431,27 +447,20 @@
         for p in range(2):
             sums[at + p, :] = var[2 + 2 * p, :width]
 
-    mw, me = roles(m1[...], m2[:MSG, :])
-    fw, fe = roles(f1[...], f2[:MSG, :])
-    mw, me, fw, fe = mw, me, fw, fe
+    mw, me = roles(m1[...], padded(m2[...], pad))
+    fw, fe = roles(f1[...], padded(f2[...], pad))
     hi = rows - (pad - LANES)
+    last = LANES - 1
     lane = lax.broadcasted_iota(jnp.int32, (MSG, LANES), 1)
-    fn_end, fn_lo, fn_hi = fn[:, width:], fn[:, :LANES], fn[:, width - LANES : width]
-    fs_end, fs_lo, fs_hi = fs[:, width:], fs[:, :LANES], fs[:, width - LANES : width]
-    down = lambda x: rolled(x, 2, 0)
-    up = lambda x: rolled(x, -2, 0)
-
-    def ended(msg, north, north_lane, south, south_lane):
-        block = msg[:, pad - LANES :]
-        block = jnp.where(lane == hi, rolled(north, hi - north_lane, 1), block)
-        block = jnp.where(lane == LANES - 1, rolled(south, LANES - 1 - south_lane, 1), block)
-        return jnp.concatenate([msg[:, : pad - LANES], block], axis=1)
-
-    last = LANES - 1
-    low_w = ended(fw, down(fn_end), last, fs_end, last)
-    high_w = ended(mw, fn_lo, 0, up(fs_lo), 0)
-    low_e = ended(me, down(fn_hi), last, fs_hi, last)
-    high_e = ended(fe, fn_end, 0, up(fs_end), 0)
+
+    def ended(msg, block, at):
+        end = msg[:, pad - LANES :]
+        end = jnp.where(lane == hi, rolled(fn[:, block : block + LANES], hi - at, 1), end)
+        end = jnp.where(lane == last, rolled(fs[:, block : block + LANES], last - at, 1), end)
+        return jnp.concatenate([msg[:, : pad - LANES], end], axis=1)
+
+    low_w, high_w = ended(fw, width, last), ended(mw, 0, 0)
+    low_e, high_e = ended(me, width - LANES, last), ended(fe, width, 0)
     row = lax.broadcasted_iota(jnp.int32, (8, pad), 1).astype(F32) + first
     ax = metric(jnp.minimum(row, first + rows), total)
     for low, high, out, at in ((low_w, high_w, w_out, 4), (low_e, high_e, e_out, 5)):
@@ -461,20 +470,22 @@
         for p in range(2):
             sums[at, p * pad : (p + 1) * pad] = var[2 + 2 * p, :]
     sums[6:, :] = jnp.zeros((2, width), F32)
-
-
-def rim(rows, m1, m2, f1, f2, mn, ms, fn, fs, after):
+    tail[:8, :] = late[...]
+    tail[8:, :] = sums[...]
+
+
+def rim(rows, m1, m2, f1, f2, mn, ms, fn, fs, late):
     row = pltpu.VMEM((48, mn.shape[1]), F32)
     col = pltpu.VMEM((48, m1.shape[1]), F32)
     sums = pltpu.VMEM((8, mn.shape[1] - LANES), F32)
     return pl.pallas_call(
         functools.partial(rim_kernel, rows),
-        out_shape=(row, row, col, col, sums),
+        out_shape=(row, row, col, col, sums, pltpu.VMEM((16, mn.shape[1] - LANES), F32)),
         in_specs=[pl.BlockSpec(memory_space=pltpu.VMEM)] * 9,
-        out_specs=[pl.BlockSpec(memory_space=pltpu.VMEM)] * 5,
+        out_specs=[pl.BlockSpec(memory_space=pltpu.VMEM)] * 6,
         compiler_params=PARAMS,
         name="rim",
-    )(*map(vmem, (after, m2, m1, f2, f1, mn, ms, fn, fs)))
+    )(*map(vmem, (late, m2, m1, f2, f1, mn, ms, fn, fs)))
 
 
 def prepare_kernel(e1_in, q, d, m, ss, sn, sw, se, du, dv, base, coef, e1, cols):
@@ -539,18 +550,70 @@
     return (DRAG * (s * lax.rsqrt(s))) * recip(d)
 
 
-def second_kernel(
-    du, dv, base, coef, d, m, mine, other, ss, sn, sw, se, eta_out, fric_out, eta, fric, cols, sems
-):
-    kdev, _, rows, width = eta.shape
+def sweep_tile(row, size, r, r_north, du, dv, base, coef, m, turned, ws, last_v, top):
+    kdev, width = du.shape[0], du.shape[3]
+    here = pl.ds(row, size)
+    edges = turned[here, :]
+    md = m[here, :]
+    coef_u, coef_v = coef[0, here, :], coef[1, here, :]
+    r2u = r + east(r)
+    r2v = r + r_north
+    squ, sqv = r2u * r2u, r2v * r2v
+    lane = lax.broadcasted_iota(jnp.int32, (size, LANES), 1)
+    last = LANES - 1
+
+    def with_east(u, k):
+        block = jnp.where(lane == last, rolled(edges, last - k, 1), u[:, width - LANES :])
+        return jnp.concatenate([u[:, : width - LANES], block], axis=1)
+
+    def from_west(u, k):
+        u = rolled(u, 1, 1)
+        block = jnp.where(lane == 0, rolled(edges, -k, 1), u[:, :LANES])
+        return jnp.concatenate([block, u[:, LANES:]], axis=1)
+
+    planes, out_v = {}, {}
+    for c in range(kdev):
+        w2 = 2.0 * ws[c]
+        gu = coef_u * recip(squ + w2 * w2)
+        gv = coef_v * recip(sqv + w2 * w2)
+        u = flux(du[c, 0, here, :], du[c, 1, here, :], gu, gu * r2u, w2)
+        v = flux(dv[c, 0, here, :], dv[c, 1, here, :], gv, gv * r2v, w2)
+        for p in range(2):
+            up, vp = with_east(u[p], 4 + 2 * p + c), v[p]
+            if top is not None:
+                vp = jnp.concatenate([vp[:-1], top(c, p, vp[-1:])], axis=0)
+            uw = from_west(up, 2 * p + c)
+            vs = jnp.concatenate([last_v[c, p], vp[:-1]], axis=0)
+            out_v[c, p] = vp[-1:]
+            planes[c, p] = base[c, p, here, :] - md * ((up - uw) + (vp - vs))
+    return planes, out_v
+
+
+def pairs(kdev):
+    return [(c, p) for c in range(kdev) for p in range(2)]
+
+
+def half_rate(var, rims, turned, d, row, low, half):
+    here = pl.ds(row, half)
+    edges = turned[here, :]
+    width = var.shape[1]
+    index = lax.broadcasted_iota(jnp.int32, (8, width), 0)
+    first = jnp.where(low & (index == 0), rims[1:2], var[:8])
+    final = jnp.where(jnp.logical_not(low) & (index == 7), rims[2:3], var[half - 8 :])
+    var = jnp.concatenate([first, var[8 : half - 8], final], axis=0)
+    lane = lax.broadcasted_iota(jnp.int32, (half, LANES), 1)
+    left = jnp.where(lane == 0, rolled(edges, -8, 1), var[:, :LANES])
+    right = jnp.where(lane == LANES - 1, rolled(edges, LANES - 1 - 9, 1), var[:, width - LANES :])
+    return rate(jnp.concatenate([left, var[:, LANES : width - LANES], right], axis=1), d[here, :])
+
+
+def own_kernel(du, dv, base, coef, d, m, mine, rims_ref, ss, sn, sw, se, eta, fric, vs_out, vn_out, turned, cols):
+    kdev, _, half, width = eta.shape
     pad = sw.shape[1]
-    size = 16
     ws = omegas(kdev)
-    half = rows // 2
     core = lax.rem(lax.axis_index("cons"), 2)
-    fric[pl.ds(pl.multiple_of(core * half, 8), half), :] = mine[:half, :]
-    fric[pl.ds(pl.multiple_of((1 - core) * half, 8), half), :] = other[:half, :]
-    rims = mine[half:, :] + other[half:, :]
+    low = core == 0
+    rims = rims_ref[...]
 
     def edge(strip, var_a, var_b):
         zr, zi, dep, ca = (strip[8 * k : 8 * k + 8, :] for k in range(4))
@@ -566,90 +629,139 @@
     north = edge(sn, wide(rims[2:3]), wide(rims[3:4]))
     west = edge(sw, rims[4:5, :pad], rims[4:5, pad : 2 * pad])
     east_ = edge(se, rims[5:6, :pad], rims[5:6, pad : 2 * pad])
-
     for p in range(2):
         cols[2 * p : 2 * p + 2, :] = west[p][2:4]
         cols[4 + 2 * p : 6 + 2 * p, :] = east_[p][2:4]
+        for c in range(kdev):
+            vs_out[2 * c + p : 2 * c + p + 1, :] = south[p][2 + c : 3 + c, :width]
+            vn_out[2 * c + p : 2 * c + p + 1, :] = north[p][2 + c : 3 + c, :width]
     cols[8:9, :] = rims[4:5, pad : 2 * pad]
     cols[9:10, :] = rims[5:6, :pad]
-    turned = cols[...].T
-
-    lane = lax.broadcasted_iota(jnp.int32, (rows, LANES), 1)
-    left, right = slice(0, LANES), slice(width - LANES, width)
-    last = LANES - 1
-    fric[0:1, :] = rims[1:2]
-    fric[rows - 1 : rows, :] = rims[2:3]
-    fric[:, left] = jnp.where(lane == 0, rolled(turned[:rows], -8, 1), fric[:, left])
-    fric[:, right] = jnp.where(lane == last, rolled(turned[:rows], last - 9, 1), fric[:, right])
-    for at in range(0, rows, size):
-        fric[at : at + size, :] = rate(fric[at : at + size, :], d[at : at + size, :])
-    copies = [pltpu.make_async_copy(fric, fric_out, sems.at[0])]
-    copies[0].start()
-
-    lane = lax.broadcasted_iota(jnp.int32, (size, LANES), 1)
-    last_v = [None] * (2 * kdev)
+    turned[...] = cols[...].T
+
+    first = pl.multiple_of(core * half, 8)
+    fric[...] = half_rate(mine[...], rims, turned, d, first, low, half)
+    size = 24
+    last_v = {(c, p): jnp.where(low, vs_out[2 * c + p : 2 * c + p + 1, :], 0.0) for c, p in pairs(kdev)}
+
+    def top(c, p, own):
+        return jnp.where(low, 0.0, vn_out[2 * c + p : 2 * c + p + 1, :])
+
+    for at in range(0, half, size):
+        r, rn = tile_rows(fric, at, size, min(at + size, half - 8))
+        planes, last_v = sweep_tile(
+            pl.multiple_of(first + at, 8), size, r, rn, du, dv, base, coef, m, turned, ws, last_v,
+            top if at + size == half else None,
+        )
+        for c, p in pairs(kdev):
+            eta[c, p, at : at + size, :] = planes[c, p]
+
+
+def own_half(du, dv, base, coef, d, m, mine, rims, ss, sn, sw, se):
+    kdev, _, rows, width = du.shape
+    pad = sw.shape[1]
+    args = (du, dv, base, coef, d, m, mine, rims, ss, sn, sw, se)
+    line = pltpu.VMEM((8, width), F32)
+    return pl.pallas_call(
+        own_kernel,
+        out_shape=(
+            pltpu.VMEM((kdev, 2, rows // 2, width), F32),
+            pltpu.VMEM((rows // 2, width), F32),
+            line,
+            line,
+            pltpu.VMEM((pad, LANES), F32),
+        ),
+        in_specs=[pl.BlockSpec(memory_space=pltpu.VMEM)] * len(args),
+        out_specs=[pl.BlockSpec(memory_space=pltpu.VMEM)] * 5,
+        scratch_shapes=[pltpu.VMEM((LANES, pad), F32)],
+        compiler_params=PARAMS,
+        name="own_half",
+    )(*map(vmem, args))
+
+
+def other_kernel(
+    du, dv, base, coef, d, m, other, rims, eta_own, fric_own, vs, vn, turned,
+    eta_out, fric_out, eta, fric, fixed, sems,
+):
+    kdev, _, half, width = eta.shape
+    ws = omegas(kdev)
+    core = lax.rem(lax.axis_index("cons"), 2)
+    own_low = core == 0
+    own, first = pl.multiple_of(core * half, 8), pl.multiple_of((1 - core) * half, 8)
+    copies = []
+
+    def put(src, dst):
+        copy = pltpu.make_async_copy(src, dst, sems.at[len(copies)])
+        copy.start()
+        copies.append(copy)
+
+    skip = pl.multiple_of(core * 8, 8)
+    put(
+        eta_own.at[:, :, pl.ds(skip, half - 8), :],
+        eta_out.at[:, :, pl.ds(pl.multiple_of(own + skip, 8), half - 8), :],
+    )
+    put(fric_own, fric_out.at[pl.ds(own, half), :])
+    fric[pl.ds(own, half), :] = fric_own[...]
+    fric[pl.ds(first, half), :] = half_rate(other[...], rims[...], turned, d, first, jnp.logical_not(own_low), half)
+    put(fric.at[pl.ds(first, half), :], fric_out.at[pl.ds(first, half), :])
+
+    r, rn = tile_rows(fric, half - 8, 8, half)
+    r2 = r + rn
+    between = {}
     for c in range(kdev):
+        w2 = 2.0 * ws[c]
+        g = coef[1, half - 8 : half, :] * recip(r2 * r2 + w2 * w2)
+        v = flux(dv[c, 0, half - 8 : half, :], dv[c, 1, half - 8 : half, :], g, g * r2, w2)
         for p in range(2):
-            last_v[2 * c + p] = south[p][2 + c : 3 + c, :width]
-    for at in range(0, rows, size):
-        nxt = min(at + size, rows - 8)
-        here = slice(at, at + size)
-        edges = turned[here]
-        md = m[here, :]
-        rd, rn = tile_rows(fric, at, size, nxt)
-        coef_u, coef_v = coef[0, here, :], coef[1, here, :]
-        r2u = rd + east(rd)
-        r2v = rd + rn
-        squ, sqv = r2u * r2u, r2v * r2v
-
-        def with_east(u, k):
-            block = jnp.where(lane == last, rolled(edges, last - k, 1), u[:, right])
-            return jnp.concatenate([u[:, : width - LANES], block], axis=1)
-
-        def from_west(u, k):
-            u = rolled(u, 1, 1)
-            block = jnp.where(lane == 0, rolled(edges, -k, 1), u[:, left])
-            return jnp.concatenate([block, u[:, LANES:]], axis=1)
-
-        for c in range(kdev):
-            w2 = 2.0 * ws[c]
-            gu = coef_u * recip(squ + w2 * w2)
-            gv = coef_v * recip(sqv + w2 * w2)
-            ur, ui = flux(du[c, 0, here, :], du[c, 1, here, :], gu, gu * r2u, w2)
-            vr, vi = flux(dv[c, 0, here, :], dv[c, 1, here, :], gv, gv * r2v, w2)
-            ur, ui = with_east(ur, 4 + c), with_east(ui, 6 + c)
-            if at + size == rows:
-                vr = jnp.concatenate([vr[:-1], north[0][2 + c : 3 + c, :width]], axis=0)
-                vi = jnp.concatenate([vi[:-1], north[1][2 + c : 3 + c, :width]], axis=0)
-            uwr, uwi = from_west(ur, c), from_west(ui, 2 + c)
-            vsr = jnp.concatenate([last_v[2 * c], vr[:-1]], axis=0)
-            vsi = jnp.concatenate([last_v[2 * c + 1], vi[:-1]], axis=0)
-            last_v[2 * c], last_v[2 * c + 1] = vr[-1:], vi[-1:]
-            eta[c, 0, here, :] = base[c, 0, here, :] - md * ((ur - uwr) + (vr - vsr))
-            eta[c, 1, here, :] = base[c, 1, here, :] - md * ((ui - uwi) + (vi - vsi))
-        copies.append(
-            pltpu.make_async_copy(eta.at[:, :, here, :], eta_out.at[:, :, here, :], sems.at[len(copies)])
+            between[c, p] = v[p][7:8]
+    index = lax.broadcasted_iota(jnp.int32, (8, width), 0)
+    at_face = index == jnp.where(own_low, 7, 0)
+    sign = jnp.where(own_low, -1.0, 1.0)
+    local = pl.ds(pl.multiple_of((1 - core) * (half - 8), 8), 8)
+    border = pl.ds(pl.multiple_of(half - 8 + 8 * core, 8), 8)
+    md = m[border, :]
+    for c, p in pairs(kdev):
+        fixed[c, p] = eta_own[c, p, local, :] + jnp.where(at_face, sign * (md * between[c, p]), 0.0)
+    put(fixed, eta_out.at[:, :, border, :])
+
+    size = 24
+    rows = 2 * half
+    last_v = {(c, p): jnp.where(own_low, between[c, p], vs[2 * c + p : 2 * c + p + 1, :]) for c, p in pairs(kdev)}
+
+    def top(c, p, own_v):
+        return jnp.where(own_low, vn[2 * c + p : 2 * c + p + 1, :], own_v)
+
+    for at in range(0, half, size):
+        row = pl.multiple_of(first + at, 8)
+        r = fric[pl.ds(row, size), :]
+        after = fric[pl.ds(pl.multiple_of(jnp.minimum(row + size, rows - 8), 8), 8), :]
+        rn = jnp.concatenate([r[1:], after[0:1]], axis=0)
+        planes, last_v = sweep_tile(
+            row, size, r, rn, du, dv, base, coef, m, turned, ws, last_v, top if at + size == half else None
         )
-        copies[-1].start()
+        for c, p in pairs(kdev):
+            eta[c, p, at : at + size, :] = planes[c, p]
+        put(eta.at[:, :, at : at + size, :], eta_out.at[:, :, pl.ds(row, size), :])
     for copy in copies:
         copy.wait()
 
 
-def second_sweep(du, dv, base, coef, d, m, mine, other, ss, sn, sw, se):
-    args = (du, dv, base, coef, d, m, mine, other, ss, sn, sw, se)
-    return pl.pallas_call(
-        second_kernel,
+def other_half(du, dv, base, coef, d, m, other, rims, eta_own, fric_own, vs, vn, turned):
+    kdev, _, rows, width = du.shape
+    args = (du, dv, base, coef, d, m, other, rims, eta_own, fric_own, vs, vn, turned)
+    return pl.pallas_call(
+        other_kernel,
         out_shape=(jax.ShapeDtypeStruct(du.shape, F32), jax.ShapeDtypeStruct(d.shape, F32)),
         in_specs=[pl.BlockSpec(memory_space=pltpu.VMEM)] * len(args),
         out_specs=[pl.BlockSpec(memory_space=pltpu.HBM)] * 2,
         scratch_shapes=[
-            pltpu.VMEM(du.shape, F32),
+            pltpu.VMEM((kdev, 2, rows // 2, width), F32),
             pltpu.VMEM(d.shape, F32),
-            pltpu.VMEM((LANES, sw.shape[1]), F32),
-            pltpu.SemaphoreType.DMA((1 + d.shape[0] // 16,)),
+            pltpu.VMEM((kdev, 2, 8, width), F32),
+            pltpu.SemaphoreType.DMA((4 + rows // 2 // 24,)),
         ],
         compiler_params=PARAMS,
-        name="second_sweep",
+        name="other_half",
     )(*map(vmem, args))
 
 
@@ -662,7 +774,8 @@
     ntx, nty, ncons = (lax.axis_size(a) for a in ("tx", "ty", "cons"))
     fields = (elevation, equilibrium, depth, land_mask, friction_prev)
     m2, m1 = pack_columns(*fields)
-    elev, equil, depth, mask, fric, mn, ms = pack(*fields, m1)
+    elev, equil, depth, mask, fric = elevation, equilibrium, depth, land_mask, friction_prev
+    mask, mn, ms = pack(*fields, m1)
     f2 = lax.ppermute(m2, "tx", [(i, (i - 1 if i % 2 == 0 else i + 1) % ntx) for i in range(ntx)])
     f1 = swapped(m1, "tx", 1)
     e1, send, keep = first_sweep(elev, equil, depth, mask, fric, m1)
@@ -673,18 +786,20 @@
     else:
         fn = lax.ppermute(ms, "ty", [(i, i - 1) for i in range(1, nty)])
         fs = lax.ppermute(mn, "ty", [(i, i + 1) for i in range(nty - 1)])
-    left, right = halves(recv, keep, my)
-    ss, sn, sw, se, rims = rim(rows, m1, m2, f1, f2, mn, ms, fn, fs, left)
+    first, second, late = cut_sum(recv, keep, my)
+    ss, sn, sw, se, rims, tail = rim(rows, m1, m2, f1, f2, mn, ms, fn, fs, late)
     prepared = prepare(e1, equil, depth, mask, ss, sn, sw, se)
-    parts, bit = [(left, right, rims)], 2
-    if bit < ncons:
-        parts.append(tuple(swapped(x, "cons", bit) for x in parts[0]))
+    pieces = (first, second, tail)
+    partner = [swapped(x, "cons", 2) for x in pieces]
+    others = [swapped(rims, "cons", k) for k in range(1, ncons) if k != 2]
+    mine, rims = joined(pieces, partner, others, prepared[2])
+    bit = 4
+    while bit < ncons:
+        mine = added(mine, swapped(mine, "cons", bit))
         bit *= 2
-    sums = joined(parts, prepared[2])
-    while bit < ncons:
-        sums = added(sums, swapped(sums, "cons", bit))
-        bit *= 2
-    return second_sweep(*prepared, depth, mask, sums, swapped(sums, "cons", 1), ss, sn, sw, se)
+    other = swapped(mine, "cons", 1)
+    fields = (*prepared, depth, mask)
+    return other_half(*fields, other, rims, *own_half(*fields, mine, rims, ss, sn, sw, se))
 
 
 def solution(mesh):

time: 24.9 us -> 23.7 us (0.952)
  Pallas kernels: 9.74 us -> 7.85 us
  starting transfers between devices: 10.5 us -> 11.5 us
  waiting for transfers between devices: 3.8 us -> 3.42 us
    ppermute x7 -> x9, starting transfers between devices: 5.38 us -> 9.03 us  [swapped(): lax.ppermute(x, axis, [(i, i ^ bit) for i in range(lax.axis_size(axis))])]
    ppermute x1, starting transfers between devices: 5.11 us -> 2.47 us  [body(): lax.ppermute(m2, 'tx', [(i, (i - 1 if i % 2 == 0 else i + 1) % ntx) for i...]
    pallas_call x5 -> x6, Pallas kernels: 6.2 us -> 4.38 us  [the longest x1 2.01 us: pack_columns(): pl.pallas_call(pack_columns_kernel, out_shape=(pltpu.VMEM((MSG, rows), F3...]
    ppermute x7 -> x9, waiting for transfers between devices: 3.79 us -> 2.59 us  [swapped(): lax.ppermute(x, axis, [(i, i ^ bit) for i in range(lax.axis_size(axis))])]
    ppermute x1, waiting for transfers between devices: 0.01 us -> 0.83 us  [body(): lax.ppermute(m2, 'tx', [(i, (i - 1 if i % 2 == 0 else i + 1) % ntx) for i...]
  transfers between devices with their start and end apart: 8 -> 10, of which waited for: 3 -> 4; matrix products, arithmetic and copies ran while one was open for 0% -> 0% of each run, Pallas kernels for 22% -> 18%
where the time goes in v2:
time: 23.7 us; the launch traced here: 23.6 us
  starting transfers between devices  11.5 us (49%)
  Pallas kernels  7.85 us (33%)
  waiting for transfers between devices  3.42 us (14%)
  between operations  0.76 us (3%)
    ppermute x9, starting transfers between devices, swapped(): lax.ppermute(x, axis, [(i, i ^ bit) for i in range(lax.axis_size(axis))])  9.03 us
    ppermute x9, waiting for transfers between devices, swapped(): lax.ppermute(x, axis, [(i, i ^ bit) for i in range(lax.axis_size(axis))])  2.59 us
    ppermute x1, starting transfers between devices, body(): lax.ppermute(m2, 'tx', [(i, (i - 1 if i % 2 == 0 else i + 1) % ntx) for i...  2.47 us
    pallas_call x1, Pallas kernels, first_sweep(): pl.pallas_call(first_kernel, out_shape=(pltpu.VMEM(e.shape, F32), half, h...  2.1 us
    pallas_call x1, Pallas kernels, pack_columns(): pl.pallas_call(pack_columns_kernel, out_shape=(pltpu.VMEM((MSG, rows), F3...  2.01 us
    pallas_call x1, Pallas kernels, other_half(): pl.pallas_call(other_kernel, out_shape=(jax.ShapeDtypeStruct(du.shape, F3...  1.49 us
    pallas_call x1, Pallas kernels, prepare(): pl.pallas_call(prepare_kernel, out_shape=(plane, plane, plane, pltpu.VMEM...  0.96 us
    ppermute x1, waiting for transfers between devices, body(): lax.ppermute(m2, 'tx', [(i, (i - 1 if i % 2 == 0 else i + 1) % ntx) for i...  0.83 us
  transfers between devices with their start and end apart: 10, of which 4 were waited for; matrix products, arithmetic and copies ran while one was open for 0% of the time, Pallas kernels for 18%

profile of v2, /device:TPU:0, one launch (start us, length us, event | category | flops | bytes accessed | tf_op | source)
XLA Modules:
  0.0 23.6 jit_solution(7504640090766961862)
XLA Ops:
  0.6 0.0 copy-start.1
  0.6 0.0 copy-start
  0.7 0.0 copy-start.3
  0.7 0.0 copy-start.2
  0.7 0.0 copy-start.4
  0.7 2.0 %pack_columns.1 = (f32[16,144]{1,0:T(8,128)S(1)}, f32[16,256]{1,0:T(8,128)S(1)}) custom-call(f32[2,2,144,512]{3,2,1,0:T(8,128)} %e.3, f32[2,2,144,512]{3,2,1,0:T(8,128)} %q.5, f32[144,512]{1,0:T(8,128)} %d.9, s32[144,512]{1,0:T(8,128)} %ints.1, f32[144,512]{1,0:T(8,128)} %r.3), custom_call_target="tpu_custom_call" | custom-call | tf_op jit(solution)/shard_map/pack_columns/pallas_call | solution.py:133
  2.7 3.1 %collective-permute-start.1 = (f32[16,256]{1,0:T(8,128)S(1)}, f32[16,256]{1,0:T(8,128)S(1)}, u32[]{:S(2)}, u32[]{:S(2)}) collective-permute-start(f32[16,256]{1,0:T(8,128)S(1)} %get-tuple-element.34.after.m1), channel_id=1, source_target_pairs={{0,1},{1,0},{2,3},{3,2},{4,5},{5,4},{6,7},{7,6},{8,9},{9,8},{10,11... | collective-permute-start | bytes 49160 | tf_op jit(solution)/shard_map/ppermute | solution.py:769
  5.8 2.5 %collective-permute-start = (f32[16,144]{1,0:T(8,128)S(1)}, f32[16,144]{1,0:T(8,128)S(1)}, u32[]{:S(2)}, u32[]{:S(2)}) collective-permute-start(f32[16,144]{1,0:T(8,128)S(1)} %get-tuple-element.37.m2), channel_id=1, source_target_pairs={{0,3},{1,2},{2,1},{3,0},{4,7},{5,6},{6,5},{7,4},{8,11},{9,10},{10,... | collective-permute-start | bytes 27656 | tf_op jit(solution)/shard_map/ppermute | solution.py:779
  8.3 0.0 copy-done.1
  8.3 0.0 copy-done
  8.3 0.0 copy-done.3
  8.3 0.0 copy-done.2
  8.3 0.0 copy-done.4
  8.3 0.1 pack.1
  8.4 2.1 %first_sweep.1 = (f32[2,2,144,512]{3,2,1,0:T(8,128)S(1)}, f32[72,512]{1,0:T(8,128)S(1)}, f32[72,512]{1,0:T(8,128)S(1)}) custom-call(f32[2,2,144,512]{3,2,1,0:T(8,128)S(1)} %copy-done.2, f32[2,2,144,512]{3,2,1,0:T(8,128)S(1)} %copy-done, f32[144,512]{1,0:T(8,128)S(1)} %copy-done.1, f32[144,512]{1,0:T(8,128)S(1)} %get-tuple-element.35.mask.m, ...), custom_call_target="tpu_custom_call" | custom-call | flops 23592960 | bytes 47185920 | tf_op jit(solution)/shard_map/first_sweep/pallas_call | solution.py:260
  10.5 0.8 %collective-permute-done.f2 = f32[16,144]{1,0:T(8,128)S(1)} collective-permute-done((f32[16,144]{1,0:T(8,128)S(1)}, f32[16,144]{1,0:T(8,128)S(1)}, u32[]{:S(2)}, u32[]{:S(2)}) %collective-permute-start) | collective-permute-done | bytes 9248 | tf_op jit(solution)/shard_map/ppermute | solution.py:779
  11.3 0.0 collective-permute-done.1.f1
  11.3 0.1 merge.1
  11.4 0.0 collective-permute-start.2
  11.4 1.6 %collective-permute-start.3 = (f32[16,640]{1,0:T(8,128)S(1)}, f32[16,640]{1,0:T(8,128)S(1)}, u32[]{:S(2)}, u32[]{:S(2)}) collective-permute-start(f32[16,640]{1,0:T(8,128)S(1)} %get-tuple-element.43.after), channel_id=1, source_target_pairs={{0,4},{4,0},{1,5},{5,1},{2,6},{6,2},{3,7},{7,3},{8,12},{12,8},{9,1... | collective-permute-start | bytes 122888 | tf_op jit(solution)/shard_map/ppermute | solution.py:769
  13.0 0.0 collective-permute-done.2.a
  13.0 1.6 %collective-permute-start.4 = (f32[32,512]{1,0:T(8,128)S(1)}, f32[32,512]{1,0:T(8,128)S(1)}, u32[]{:S(2)}, u32[]{:S(2)}) collective-permute-start(f32[32,512]{1,0:T(8,128)S(1)} %get-tuple-element.55.refs_0_), channel_id=1, source_target_pairs={{0,16},{8,24},{16,0},{24,8},{1,17},{9,25},{17,1},{25,9},{2,18},{10... | collective-permute-start | bytes 196616 | tf_op jit(solution)/shard_map/ppermute | solution.py:769
  14.6 0.5 %collective-permute-start.5 = (f32[32,512]{1,0:T(8,128)S(1)}, f32[32,512]{1,0:T(8,128)S(1)}, u32[]{:S(2)}, u32[]{:S(2)}) collective-permute-start(f32[32,512]{1,0:T(8,128)S(1)} %get-tuple-element.56.refs_1_), channel_id=1, source_target_pairs={{0,16},{8,24},{16,0},{24,8},{1,17},{9,25},{17,1},{25,9},{2,18},{10... | collective-permute-start | bytes 196616 | tf_op jit(solution)/shard_map/ppermute | solution.py:769
  15.1 0.4 %collective-permute-done.3.fn_ref.fs_ref = f32[16,640]{1,0:T(8,128)S(1)} collective-permute-done((f32[16,640]{1,0:T(8,128)S(1)}, f32[16,640]{1,0:T(8,128)S(1)}, u32[]{:S(2)}, u32[]{:S(2)}) %collective-permute-start.3) | collective-permute-done | bytes 40992 | tf_op jit(solution)/shard_map/ppermute | solution.py:769
  15.5 0.3 %rim.1 = (f32[48,640]{1,0:T(8,128)S(1)}, f32[48,640]{1,0:T(8,128)S(1)}, f32[48,256]{1,0:T(8,128)S(1)}, f32[48,256]{1,0:T(8,128)S(1)}, f32[8,512]{1,0:T(8,128)S(1)}, /*index=5*/f32[16,512]{1,0:T(8,128)S(1)}) custom-call(f32[8,512]{1,0:T(8,128)S(1)} %get-tuple-element.44.late, f32[16,144]{1,0:T(8,128)S(1)} %get-tuple-element.37.m2, ...), custom_call_target="tpu_custom_call" | custom-call | tf_op jit(solution)/shard_map/rim/pallas_call | solution.py:481
  15.8 1.6 %collective-permute-start.6 = (f32[16,512]{1,0:T(8,128)S(1)}, f32[16,512]{1,0:T(8,128)S(1)}, u32[]{:S(2)}, u32[]{:S(2)}) collective-permute-start(f32[16,512]{1,0:T(8,128)S(1)} %get-tuple-element.57.refs_2_), channel_id=1, source_target_pairs={{0,16},{8,24},{16,0},{24,8},{1,17},{9,25},{17,1},{25,9},{2,18},{10... | collective-permute-start | bytes 98312 | tf_op jit(solution)/shard_map/ppermute | solution.py:769
  17.4 0.0 collective-permute-start.8
  17.4 0.6 %collective-permute-start.7 = (f32[8,512]{1,0:T(8,128)S(1)}, f32[8,512]{1,0:T(8,128)S(1)}, u32[]{:S(2)}, u32[]{:S(2)}) collective-permute-start(f32[8,512]{1,0:T(8,128)S(1)} %get-tuple-element.58), channel_id=1, source_target_pairs={{0,8},{8,0},{16,24},{24,16},{1,9},{9,1},{17,25},{25,17},{2,10},{10... | collective-permute-start | bytes 49160 | tf_op jit(solution)/shard_map/ppermute | solution.py:769
  18.0 1.0 %prepare.1 = (f32[2,2,144,512]{3,2,1,0:T(8,128)S(1)}, f32[2,2,144,512]{3,2,1,0:T(8,128)S(1)}, f32[2,2,144,512]{3,2,1,0:T(8,128)S(1)}, f32[2,144,512]{2,1,0:T(8,128)S(1)}) custom-call(f32[2,2,144,512]{3,2,1,0:T(8,128)S(1)} %get-tuple-element.36.e1_in, f32[2,2,144,512]{3,2,1,0:T(8,128)S(1)} %copy-done, f32[144,512]{1,0:T(8,128)S(1)} %copy-done.1, ...), custom_call_target="tpu_custom_call" | custom-call | flops 11796480 | bytes 47185920 | tf_op jit(solution)/shard_map/prepare/pallas_call | solution.py:536
  19.0 1.6 %collective-permute-done.8.refs_7_ = f32[8,512]{1,0:T(8,128)S(1)} collective-permute-done((f32[8,512]{1,0:T(8,128)S(1)}, f32[8,512]{1,0:T(8,128)S(1)}, u32[]{:S(2)}, u32[]{:S(2)}) %collective-permute-start.8) | collective-permute-done | bytes 16416 | tf_op jit(solution)/shard_map/ppermute | solution.py:769
  20.6 0.0 collective-permute-done.7.refs_6_
  20.6 0.0 collective-permute-done.6.refs_5_
  20.6 0.0 collective-permute-done.4.refs_3_
  20.6 0.0 collective-permute-done.5.refs_4_
  20.6 0.1 collective-permute-start.9
  20.7 0.7 %own_half.1 = (f32[2,2,72,512]{3,2,1,0:T(8,128)S(1)}, f32[72,512]{1,0:T(8,128)S(1)}, f32[8,512]{1,0:T(8,128)S(1)}, f32[8,512]{1,0:T(8,128)S(1)}, f32[256,128]{1,0:T(8,128)S(1)}) custom-call(f32[2,2,144,512]{3,2,1,0:T(8,128)S(1)} %get-tuple-element.51.du, f32[2,2,144,512]{3,2,1,0:T(8,128)S(1)} %get-tuple-element.52.dv, ...), custom_call_target="tpu_custom_call" | custom-call | tf_op jit(solution)/shard_map/own_half/pallas_call | solution.py:665
  21.5 0.6 %collective-permute-done.9.other = f32[72,512]{1,0:T(8,128)S(1)} collective-permute-done((f32[72,512]{1,0:T(8,128)S(1)}, f32[72,512]{1,0:T(8,128)S(1)}, u32[]{:S(2)}, u32[]{:S(2)}) %collective-permute-start.9) | collective-permute-done | bytes 147488 | tf_op jit(solution)/shard_map/ppermute | solution.py:769
  22.1 1.5 %other_half.1 = (f32[2,2,144,512]{3,2,1,0:T(8,128)}, f32[144,512]{1,0:T(8,128)}) custom-call(f32[2,2,144,512]{3,2,1,0:T(8,128)S(1)} %get-tuple-element.51.du, f32[2,2,144,512]{3,2,1,0:T(8,128)S(1)} %get-tuple-element.52.dv, f32[2,2,144,512]{3,2,1,0:T(8,128)S(1)} %get-tuple-element.53.after.base, f32[2,144,512]{2,1,0:T(8,128)S(1)} %get-tuple-element.54.coef, ...), custom_call_target="tpu_custom_call" | custom-call | tf_op jit(solution)/shard_map/other_half/pallas_call | solution.py:752
  (2 shorter events, 0.0 us)
Async XLA Ops:
  0.6 7.6 %copy-start.1 = (f32[144,512]{1,0:T(8,128)S(1)}, f32[144,512]{1,0:T(8,128)}, u32[]{:S(2)}) copy-start(f32[144,512]{1,0:T(8,128)} %d.9) | copy-start | bytes 884740
  0.6 7.6 %copy-start = (f32[2,2,144,512]{3,2,1,0:T(8,128)S(1)}, f32[2,2,144,512]{3,2,1,0:T(8,128)}, u32[]{:S(2)}) copy-start(f32[2,2,144,512]{3,2,1,0:T(8,128)} %q.5) | copy-start | bytes 3538948
  0.7 7.6 %copy-start.3 = (f32[144,512]{1,0:T(8,128)S(1)}, f32[144,512]{1,0:T(8,128)}, u32[]{:S(2)}) copy-start(f32[144,512]{1,0:T(8,128)} %r.3) | copy-start | bytes 884740
  0.7 7.6 %copy-start.2 = (f32[2,2,144,512]{3,2,1,0:T(8,128)S(1)}, f32[2,2,144,512]{3,2,1,0:T(8,128)}, u32[]{:S(2)}) copy-start(f32[2,2,144,512]{3,2,1,0:T(8,128)} %e.3) | copy-start | bytes 3538948
  0.7 7.6 %copy-start.4 = (s32[144,512]{1,0:T(8,128)S(1)}, s32[144,512]{1,0:T(8,128)}, u32[]{:S(2)}) copy-start(s32[144,512]{1,0:T(8,128)} %ints.1) | copy-start | bytes 884740
  2.7 8.6 %collective-permute-start.1 = (f32[16,256]{1,0:T(8,128)S(1)}, f32[16,256]{1,0:T(8,128)S(1)}, u32[]{:S(2)}, u32[]{:S(2)}) collective-permute-start(f32[16,256]{1,0:T(8,128)S(1)} %get-tuple-element.34.after.m1), channel_id=1, source_target_pairs={{0,1},{1,0},{2,3},{3,2},{4,5},{5,4},{6,7},{7,6},{8,9},{9,8},{10,11... | collective-permute-start | bytes 49160 | tf_op jit(solution)/shard_map/ppermute | solution.py:769
  5.8 5.5 %collective-permute-start = (f32[16,144]{1,0:T(8,128)S(1)}, f32[16,144]{1,0:T(8,128)S(1)}, u32[]{:S(2)}, u32[]{:S(2)}) collective-permute-start(f32[16,144]{1,0:T(8,128)S(1)} %get-tuple-element.37.m2), channel_id=1, source_target_pairs={{0,3},{1,2},{2,1},{3,0},{4,7},{5,6},{6,5},{7,4},{8,11},{9,10},{10,... | collective-permute-start | bytes 27656 | tf_op jit(solution)/shard_map/ppermute | solution.py:779
  11.4 1.6 %collective-permute-start.2 = (f32[72,512]{1,0:T(8,128)S(1)}, f32[72,512]{1,0:T(8,128)S(1)}, u32[]{:S(2)}, u32[]{:S(2)}) collective-permute-start(f32[72,512]{1,0:T(8,128)S(1)} %get-tuple-element.41), channel_id=1, source_target_pairs={{0,8},{8,0},{16,24},{24,16},{1,9},{9,1},{17,25},{25,17},{2,10},{10... | collective-permute-start | bytes 442376 | tf_op jit(solution)/shard_map/ppermute | solution.py:769
  11.4 4.1 %collective-permute-start.3 = (f32[16,640]{1,0:T(8,128)S(1)}, f32[16,640]{1,0:T(8,128)S(1)}, u32[]{:S(2)}, u32[]{:S(2)}) collective-permute-start(f32[16,640]{1,0:T(8,128)S(1)} %get-tuple-element.43.after), channel_id=1, source_target_pairs={{0,4},{4,0},{1,5},{5,1},{2,6},{6,2},{3,7},{7,3},{8,12},{12,8},{9,1... | collective-permute-start | bytes 122888 | tf_op jit(solution)/shard_map/ppermute | solution.py:769
  13.0 7.6 %collective-permute-start.4 = (f32[32,512]{1,0:T(8,128)S(1)}, f32[32,512]{1,0:T(8,128)S(1)}, u32[]{:S(2)}, u32[]{:S(2)}) collective-permute-start(f32[32,512]{1,0:T(8,128)S(1)} %get-tuple-element.55.refs_0_), channel_id=1, source_target_pairs={{0,16},{8,24},{16,0},{24,8},{1,17},{9,25},{17,1},{25,9},{2,18},{10... | collective-permute-start | bytes 196616 | tf_op jit(solution)/shard_map/ppermute | solution.py:769
  14.6 6.0 %collective-permute-start.5 = (f32[32,512]{1,0:T(8,128)S(1)}, f32[32,512]{1,0:T(8,128)S(1)}, u32[]{:S(2)}, u32[]{:S(2)}) collective-permute-start(f32[32,512]{1,0:T(8,128)S(1)} %get-tuple-element.56.refs_1_), channel_id=1, source_target_pairs={{0,16},{8,24},{16,0},{24,8},{1,17},{9,25},{17,1},{25,9},{2,18},{10... | collective-permute-start | bytes 196616 | tf_op jit(solution)/shard_map/ppermute | solution.py:769
  15.8 4.8 %collective-permute-start.6 = (f32[16,512]{1,0:T(8,128)S(1)}, f32[16,512]{1,0:T(8,128)S(1)}, u32[]{:S(2)}, u32[]{:S(2)}) collective-permute-start(f32[16,512]{1,0:T(8,128)S(1)} %get-tuple-element.57.refs_2_), channel_id=1, source_target_pairs={{0,16},{8,24},{16,0},{24,8},{1,17},{9,25},{17,1},{25,9},{2,18},{10... | collective-permute-start | bytes 98312 | tf_op jit(solution)/shard_map/ppermute | solution.py:769
  17.4 3.2 %collective-permute-start.8 = (f32[8,512]{1,0:T(8,128)S(1)}, f32[8,512]{1,0:T(8,128)S(1)}, u32[]{:S(2)}, u32[]{:S(2)}) collective-permute-start(f32[8,512]{1,0:T(8,128)S(1)} %get-tuple-element.58), channel_id=1, source_target_pairs={{0,24},{8,16},{16,8},{24,0},{1,25},{9,17},{17,9},{25,1},{2,26},{10... | collective-permute-start | bytes 49160 | tf_op jit(solution)/shard_map/ppermute | solution.py:769
  17.4 3.2 %collective-permute-start.7 = (f32[8,512]{1,0:T(8,128)S(1)}, f32[8,512]{1,0:T(8,128)S(1)}, u32[]{:S(2)}, u32[]{:S(2)}) collective-permute-start(f32[8,512]{1,0:T(8,128)S(1)} %get-tuple-element.58), channel_id=1, source_target_pairs={{0,8},{8,0},{16,24},{24,16},{1,9},{9,1},{17,25},{25,17},{2,10},{10... | collective-permute-start | bytes 49160 | tf_op jit(solution)/shard_map/ppermute | solution.py:769
  20.6 1.4 %collective-permute-start.9 = (f32[72,512]{1,0:T(8,128)S(1)}, f32[72,512]{1,0:T(8,128)S(1)}, u32[]{:S(2)}, u32[]{:S(2)}) collective-permute-start(f32[72,512]{1,0:T(8,128)S(1)} %get-tuple-element.59.mine), channel_id=1, source_target_pairs={{0,8},{8,0},{16,24},{24,16},{1,9},{9,1},{17,25},{25,17},{2,10},{10... | collective-permute-start | bytes 442376 | tf_op jit(solution)/shard_map/ppermute | solution.py:769
